TPU v7x, 32 devices: a whole 2x2x4 slice. The times are simulated.
32 devices in a mesh: scene: 2 (over x), view: 16 (over z, y, core).
Axes of the slice: x: 2, y: 2, z: 4, core: 2. Of those that a mesh axis runs over, the one named last changes fastest.
Arguments:
- latents: bfloat16 [64, 256, 1024], P(('scene', 'view')), parts along dimension 0, may hold values from -6 to 6
- mod_scale: float32 [64, 1024], P(('scene', 'view')), parts along dimension 0
- observed: bfloat16 [2048, 1024], P(('scene', 'view')), parts along dimension 0, may hold values from -6 to 6
- w_query: bfloat16 [1024, 1024], replicated, may hold values from -0.1875 to 0.1875
- w_keyval: bfloat16 [1024, 2048], replicated, may hold values from -0.1875 to 0.1875
- w_out: bfloat16 [1024, 1024], replicated, may hold values from -3 to 3
- pair_views: int32 [64, 5], P(('scene', 'view')), parts along dimension 0, may hold values from 0 to 31, as said below
- pair_count: int32 [64], P(('scene', 'view')), parts along dimension 0, may hold values from 1 to 5
- cond_views: int32 [64, 4], P(('scene', 'view')), parts along dimension 0, may hold values from 0 to 3, as said below
- cond_count: int32 [64], P(('scene', 'view')), parts along dimension 0, may hold values from 1 to 4
- obs_count: int32 [8], P('scene'), parts along dimension 0, may hold values from 128 to 256
Outputs:
- attended: bfloat16 [64, 256, 1024], P(('scene', 'view')), parts along dimension 0
There are 2 independent parts, one for each index of `scene`. A program takes and returns all parts, laid end to end along the dimension named above; an argument that names none is the same for every part. Nothing has to cross between parts.
Inputs may be any that keep to these rules, and one draw needn't show every extreme that they name: `pair_views`: slot 0 is the view itself; the slots below pair_count[v] are distinct views at most 2 places from v around the cycle of 32 views; later slots repeat v. `cond_views`: the slots below cond_count[v] are distinct observed views; later slots repeat slot 0.
All inputs are finite; a program needn't handle non-finite values.
Results may differ from a plain program's by a relative error of at most 0.004.
The roundings to bfloat16 on the way count: a program that leaves them out, or rounds other values in their place, can miss the bound.
Values may be sent and summed in bfloat16 or wider, within the bound.
A program may use at most 128 MiB of HBM per device.

v0:
```python
import jax
import jax.numpy as jnp
from jax import lax
from jax.sharding import PartitionSpec as P

HEADS = 16


def with_halo(array, sides, width):
    for axis, dim in sides:
        peers, length = (lax.axis_size(axis), array.shape[dim])
        up = [(i, (i + 1) % peers) for i in range(peers)]
        down = [(j, i) for i, j in up]
        last = lax.slice_in_dim(array, length - width, length, axis=dim)
        leading = lax.slice_in_dim(array, 0, width, axis=dim)
        before = lax.ppermute(last, axis, up)
        after = lax.ppermute(leading, axis, down)
        array = jnp.concatenate([before, array, after], axis=dim)
    return array


def normalize(rows):
    values = rows.astype(jnp.float32)
    centered = values - jnp.mean(values, axis=-1, keepdims=True)
    return centered * lax.rsqrt(jnp.mean(centered * centered, axis=-1, keepdims=True) + 1e-06)


def attend_group(query, keys, values, live, size):
    batch, rows, cols = query.shape
    count = keys.shape[1]
    q_heads = query.reshape(batch, rows, cols // size, size)
    k_heads = keys.reshape(batch, count, cols // size, size)
    v_heads = values.reshape(batch, count, cols // size, size)
    scores = jnp.einsum(
        "bqhd,bkhd->bhqk", q_heads, k_heads, preferred_element_type=jnp.float32
    ) * size ** (-0.5)
    scores = jnp.where(live[:, None, None, :], scores, jnp.float32(-1e30))
    top = jnp.max(scores, axis=-1, keepdims=True)
    weights = jnp.exp(scores - top)
    probs = (weights / jnp.sum(weights, axis=-1, keepdims=True)).astype(jnp.bfloat16)
    mixed = jnp.einsum("bhqk,bkhd->bqhd", probs, v_heads, preferred_element_type=jnp.float32)
    return mixed.astype(jnp.bfloat16).reshape(batch, rows, cols)


def shards(
    latents,
    mod_scale,
    observed,
    w_query,
    w_keyval,
    w_out,
    pair_views,
    pair_count,
    cond_views,
    cond_count,
    obs_count,
):
    view_dev, tok_view, width = latents.shape
    slots = pair_views.shape[1]
    reach = (slots - 1) // 2
    views = view_dev * lax.axis_size("view")
    first = lax.axis_index("view") * view_dev
    obs_views = obs_count.shape[0]
    modulated = (normalize(latents) * mod_scale[:, None, :]).astype(jnp.bfloat16)
    flat = modulated.reshape(view_dev * tok_view, width)
    query = (
        jnp.dot(flat, w_query, preferred_element_type=jnp.float32)
        .astype(jnp.bfloat16)
        .reshape(view_dev, tok_view, width)
    )
    obs_local = jnp.dot(
        normalize(observed).astype(jnp.bfloat16), w_keyval, preferred_element_type=jnp.float32
    ).astype(jnp.bfloat16)
    obs_keyval = lax.all_gather(obs_local, "view", axis=0, tiled=True)
    keyval = jnp.dot(flat, w_keyval, preferred_element_type=jnp.float32).astype(jnp.bfloat16)
    keyval = keyval.reshape(view_dev, tok_view, 2 * width)
    window_kv = with_halo(keyval, (("view", 0),), reach)
    windows = jnp.stack([window_kv[index : index + slots] for index in range(view_dev)])
    windows = windows.reshape(view_dev, slots * tok_view, 2 * width)
    obs_all = jnp.broadcast_to(obs_keyval[None], (view_dev,) + obs_keyval.shape)
    keys_all = jnp.concatenate([windows, obs_all], axis=1)
    view_ids = first + jnp.arange(view_dev, dtype=jnp.int32)
    targets = (view_ids[:, None] + jnp.arange(slots, dtype=jnp.int32)[None, :] - reach) % views
    pair_live = jnp.arange(slots, dtype=jnp.int32)[None, :] < pair_count[:, None]
    window_live = jnp.any(
        (pair_views[:, None, :] == targets[:, :, None]) & pair_live[:, None, :], axis=-1
    )
    cond_live = jnp.arange(obs_views, dtype=jnp.int32)[None, :] < cond_count[:, None]
    obs_ids = jnp.arange(obs_views, dtype=jnp.int32)
    obs_live = jnp.any(
        (cond_views[:, None, :] == obs_ids[None, :, None]) & cond_live[:, None, :], axis=-1
    )
    token_live = jnp.arange(tok_view, dtype=jnp.int32)[None, :] < obs_count[:, None]
    obs_key_live = (obs_live[:, :, None] & token_live[None, :, :]).reshape(
        view_dev, obs_views * tok_view
    )
    window_key_live = jnp.repeat(window_live, tok_view, axis=1)
    live = jnp.concatenate([window_key_live, obs_key_live], axis=1)
    size = width // HEADS
    group_cols = width // 4
    outputs = []
    for group in range(4):
        low = group * group_cols
        outputs.append(
            attend_group(
                query[:, :, low : low + group_cols],
                keys_all[:, :, low : low + group_cols],
                keys_all[:, :, width + low : width + low + group_cols],
                live,
                size,
            )
        )
    heads_out = jnp.concatenate(outputs, axis=2)
    attended = jnp.dot(
        heads_out.reshape(view_dev * tok_view, width), w_out, preferred_element_type=jnp.float32
    )
    return attended.astype(jnp.bfloat16).reshape(view_dev, tok_view, width)


def solution(mesh):
    in_specs = (
        P(("scene", "view"), None, None),
        P(("scene", "view"), None),
        P(("scene", "view"), None),
        P(),
        P(),
        P(),
        P(("scene", "view"), None),
        P(("scene", "view")),
        P(("scene", "view"), None),
        P(("scene", "view")),
        P("scene"),
    )
    out_specs = P(("scene", "view"), None, None)
    return jax.shard_map(shards, mesh=mesh, in_specs=in_specs, out_specs=out_specs, check_vma=False)
```

profile of v0, /device:TPU:1, one launch (start us, length us, event | category | flops | bytes accessed | tf_op | source)
XLA Modules:
  0.0 253.2 jit_solution(518293264290757975)
XLA Ops:
  6.5 1.2 convert_reduce_fusion.1
  7.7 1.1 fusion.54
  8.9 3.9 %convolution_convert_fusion.1 = bf16[64,2048]{1,0:T(8,128)(2,1)} fusion(bf16[1024,2048]{1,0:T(8,128)(2,1)} %param.15, bf16[64,1024]{1,0:T(8,128)(2,1)} %param.13, f32[64]{0:T(128)S(1)} %add_rsqrt_fusion.1, f32[64]{0:T(128)S(1)} %broadcast_multiply_fusion.1), kind=kOutput, calls=%fused_computation.47 | convolution fusion | flops 268828672 | bytes 4588032 | tf_op jit(solution)/shard_map/dot_general | solution.py:71
  12.7 0.0 all-gather.2.cloned.1.call-update
  12.8 0.2 convert_reduce_fusion
  13.0 0.4 fusion.34
  13.4 0.4 fusion.36
  13.8 0.0 copy-start.3
  13.8 0.0 copy-start.9
  13.9 6.3 %convolution_convert_fusion = bf16[512,2048]{1,0:T(8,128)(2,1)} fusion(bf16[512,1024]{1,0:T(8,128)(2,1)S(1)} %bitcast.92, bf16[1024,2048]{1,0:T(8,128)(2,1)} %param.15), kind=kOutput, calls=%fused_computation.42 | convolution fusion | flops 2148532224 | bytes 7340032 | tf_op jit(solution)/shard_map/dot_general | solution.py:75
  20.2 0.1 collective-permute-start.1
  20.2 2.6 %collective-permute-start = (bf16[2,256,2048]{2,1,0:T(8,128)(2,1)}, bf16[2,256,2048]{2,1,0:T(8,128)(2,1)}, u32[]{:S(2)}, u32[]{:S(2)}) collective-permute-start(bf16[2,256,2048]{2,1,0:T(8,128)(2,1)} %bitcast.1), channel_id=1, source_target_pairs={{0,1},{1,2},{2,3},{3,4},{4,5},{5,6},{6,7},{7,8},{8,9},{9,10},{10,1... | collective-permute-start | bytes 6291464 | tf_op jit(solution)/shard_map/ppermute | solution.py:16
  22.8 0.1 iota_compare_fusion.1
  22.9 0.1 fusion.60
  23.0 0.1 broadcast_bitcast_fusion.1
  23.1 0.1 iota_compare_fusion.2
  23.2 0.1 and_select_fusion
  23.3 0.2 and_reduce_fusion
  23.5 0.1 broadcast_bitcast_fusion
  23.6 2.5 convolution_convert_fusion.3
  26.2 0.1 fusion.73
  26.2 0.1 copy.33
  26.4 0.1 copy.39
  26.5 0.1 copy.37
  26.7 0.1 copy.35
  26.8 0.1 lt.67
  26.9 56.4 %collective-permute-done.1 = bf16[2,256,2048]{2,1,0:T(8,128)(2,1)} collective-permute-done((bf16[2,256,2048]{2,1,0:T(8,128)(2,1)}, bf16[2,256,2048]{2,1,0:T(8,128)(2,1)}, u32[]{:S(2)}, u32[]{:S(2)}) %collective-permute-start.1) | collective-permute-done | bytes 2097184 | tf_op jit(solution)/shard_map/ppermute | solution.py:17
  83.3 6.4 %pad_maximum_fusion.1 = bf16[6,256,2048]{2,1,0:T(8,128)(2,1)} fusion(bf16[2,256,2048]{2,1,0:T(8,128)(2,1)} %collective-permute-done.1, bf16[2,256,2048]{2,1,0:T(8,128)(2,1)} %bitcast.1, bf16[2,256,2048]{2,1,0:T(8,128)(2,1)} %collective-permute-done), kind=kLoop, calls=%fused_computation.41 | loop fusion | flops 6291456 | bytes 12582912 | tf_op jit(solution)/shard_map/concatenate | solution.py:18
  89.8 10.3 %fusion.72 = (bf16[5,256,2048]{2,1,0:T(8,128)(2,1)}, bf16[5,256,2048]{2,1,0:T(8,128)(2,1)}) fusion(bf16[6,256,2048]{2,1,0:T(8,128)(2,1)} %pad_maximum_fusion.1), kind=kLoop, calls=%fused_computation.106 | loop fusion | bytes 20971520 | tf_op jit(solution)/shard_map/slice | solution.py:78
  100.0 7.9 %copy.30 = bf16[1,1280,2048]{1,2,0:T(8,128)(2,1)} copy(bf16[1,1280,2048]{2,1,0:T(8,128)(2,1)} %bitcast.83) | data formatting | bytes 10485760 | tf_op jit(solution)/shard_map/stack | solution.py:78
  107.9 7.9 %copy.31 = bf16[1,1280,2048]{1,2,0:T(8,128)(2,1)} copy(bf16[1,1280,2048]{2,1,0:T(8,128)(2,1)} %bitcast.82) | data formatting | bytes 10485760 | tf_op jit(solution)/shard_map/stack | solution.py:78
  115.8 6.4 %copy.32 = bf16[1024,2048]{0,1:T(8,128)(2,1)} copy(bf16[1024,2048]{1,0:T(8,128)(2,1)} %all-gather.2.cloned.1.call-done) | data formatting | bytes 8388608 | tf_op jit(solution)/shard_map/all_gather | solution.py:74
  122.2 6.7 %broadcast_in_dim.24 = bf16[2,1024,2048]{1,2,0:T(8,128)(2,1)} broadcast(bf16[1024,2048]{0,1:T(8,128)(2,1)} %copy.32), dimensions={1,2} | broadcast | bytes 12582912 | tf_op jit(solution)/shard_map/broadcast_in_dim | solution.py:80
  129.0 16.1 %pad_maximum_fusion = bf16[2,2304,2048]{1,2,0:T(8,128)(2,1)} fusion(bf16[2,1024,2048]{1,2,0:T(8,128)(2,1)} %broadcast_in_dim.24, bf16[1,1280,2048]{1,2,0:T(8,128)(2,1)} %copy.31, bf16[1,1280,2048]{1,2,0:T(8,128)(2,1)} %copy.30), kind=kLoop, calls=%fused_computation.4 | loop fusion | flops 56623104 | bytes 37748736 | tf_op jit(solution)/shard_map/concatenate | solution.py:81
  145.1 13.4 %fusion.71 = (bf16[2,2304,256]{1,2,0:T(8,128)(2,1)}, bf16[2,2304,256]{1,2,0:T(8,128)(2,1)}, bf16[2,2304,256]{1,2,0:T(8,128)(2,1)}, bf16[2,2304,256]{1,2,0:T(8,12...) fusion(bf16[2,2304,2048]{1,2,0:T(8,128)(2,1)} %pad_maximum_fusion), kind=kLoop, calls=%fused_computation.105 | loop fusion | bytes 37748736 | tf_op jit(solution)/shard_map/slice | solution.py:107
  158.5 10.8 %fusion.74 = (f32[2,4,256]{2,1,0:T(4,128)S(1)}, f32[2,4,256,2304]{3,2,1,0:T(8,128)}) fusion(bf16[2,256,4,64]{1,3,2,0:T(8,128)(2,1)S(1)} %bitcast.102, bf16[2,2304,4,64]{1,3,2,0:T(8,128)(2,1)} %bitcast.91, pred[2,2304]{1,0:T(4,128)(4,1)S(1)} %pad_add_fusion), kind=kOutput, calls=%fused_computation.108 | convolution fusion | flops 622856448 | bytes 21508608 | tf_op jit(solution)/shard_map/sub | solution.py:39
  169.3 10.1 %fusion.44 = bf16[2,256,4,64]{1,3,2,0:T(8,128)(2,1)S(1)} fusion(bf16[2,2304,4,64]{1,3,2,0:T(8,128)(2,1)} %bitcast.90, f32[2,4,256,2304]{3,2,1,0:T(8,128)} %get-tuple-element.20, f32[2,4,256]{2,1,0:T(4,128)S(1)} %get-tuple-element.19), kind=kOutput, calls=%fused_computation.60 | convolution fusion | flops 613548032 | bytes 21504000 | tf_op jit(solution)/shard_map/bhqk,bkhd->bqhd/dot_general | solution.py:41
  179.4 0.3 copy.40
  179.7 11.0 %fusion.77 = (f32[2,4,256]{2,1,0:T(4,128)S(1)}, f32[2,4,256,2304]{3,2,1,0:T(8,128)}) fusion(bf16[2,256,4,64]{1,3,2,0:T(8,128)(2,1)S(1)} %bitcast.101, bf16[2,2304,4,64]{1,3,2,0:T(8,128)(2,1)} %bitcast.89, pred[2,2304]{1,0:T(4,128)(4,1)S(1)} %pad_add_fusion), kind=kOutput, calls=%fused_computation.111 | convolution fusion | flops 622856448 | bytes 21508608 | tf_op jit(solution)/shard_map/sub | solution.py:39
  190.7 10.1 %fusion.41 = bf16[2,256,4,64]{1,3,2,0:T(8,128)(2,1)S(1)} fusion(bf16[2,2304,4,64]{1,3,2,0:T(8,128)(2,1)} %bitcast.88, f32[2,4,256,2304]{3,2,1,0:T(8,128)} %get-tuple-element.26, f32[2,4,256]{2,1,0:T(4,128)S(1)} %get-tuple-element.25), kind=kOutput, calls=%fused_computation.57 | convolution fusion | flops 613548032 | bytes 21504000 | tf_op jit(solution)/shard_map/bhqk,bkhd->bqhd/dot_general | solution.py:41
  200.9 0.3 copy.34
  201.2 10.8 %fusion.75 = (f32[2,4,256]{2,1,0:T(4,128)S(1)}, f32[2,4,256,2304]{3,2,1,0:T(8,128)}) fusion(bf16[2,256,4,64]{1,3,2,0:T(8,128)(2,1)S(1)} %bitcast.100, bf16[2,2304,4,64]{1,3,2,0:T(8,128)(2,1)} %bitcast.87, pred[2,2304]{1,0:T(4,128)(4,1)S(1)} %pad_add_fusion), kind=kOutput, calls=%fused_computation.109 | convolution fusion | flops 622856448 | bytes 21508608 | tf_op jit(solution)/shard_map/sub | solution.py:39
  212.0 10.1 %fusion.43 = bf16[2,256,4,64]{1,3,2,0:T(8,128)(2,1)S(1)} fusion(bf16[2,2304,4,64]{1,3,2,0:T(8,128)(2,1)} %bitcast.86, f32[2,4,256,2304]{3,2,1,0:T(8,128)} %get-tuple-element.22, f32[2,4,256]{2,1,0:T(4,128)S(1)} %get-tuple-element.21), kind=kOutput, calls=%fused_computation.59 | convolution fusion | flops 613548032 | bytes 21504000 | tf_op jit(solution)/shard_map/bhqk,bkhd->bqhd/dot_general | solution.py:41
  222.1 0.3 copy.38
  222.4 11.1 %fusion.76 = (f32[2,4,256]{2,1,0:T(4,128)S(1)}, f32[2,4,256,2304]{3,2,1,0:T(8,128)}) fusion(bf16[2,256,4,64]{1,3,2,0:T(8,128)(2,1)S(1)} %bitcast.99, bf16[2,2304,4,64]{1,3,2,0:T(8,128)(2,1)} %bitcast.85, pred[2,2304]{1,0:T(4,128)(4,1)S(1)} %pad_add_fusion), kind=kOutput, calls=%fused_computation.110 | convolution fusion | flops 622856448 | bytes 21508608 | tf_op jit(solution)/shard_map/sub | solution.py:39
  233.5 10.2 %fusion.42 = bf16[2,256,4,64]{1,3,2,0:T(8,128)(2,1)S(1)} fusion(bf16[2,2304,4,64]{1,3,2,0:T(8,128)(2,1)} %bitcast.84, f32[2,4,256,2304]{3,2,1,0:T(8,128)} %get-tuple-element.24, f32[2,4,256]{2,1,0:T(4,128)S(1)} %get-tuple-element.23), kind=kOutput, calls=%fused_computation.58 | convolution fusion | flops 613548032 | bytes 21504000 | tf_op jit(solution)/shard_map/bhqk,bkhd->bqhd/dot_general | solution.py:41
  243.7 0.3 copy.36
  244.1 2.3 convolution_convert_fusion.2
  (39 shorter events, 0.3 us)
Async XLA Ops:
  6.5 17.1 %copy-start = (bf16[1024,1024]{1,0:T(8,128)(2,1)S(1)}, bf16[1024,1024]{1,0:T(8,128)(2,1)}, u32[]{:S(2)}) copy-start(bf16[1024,1024]{1,0:T(8,128)(2,1)} %param.14) | copy-start | bytes 6291460
  6.5 6.2 %copy-start.2 = (bf16[2,256,1024]{2,1,0:T(8,128)(2,1)S(1)}, bf16[2,256,1024]{2,1,0:T(8,128)(2,1)}, u32[]{:S(2)}) copy-start(bf16[2,256,1024]{2,1,0:T(8,128)(2,1)} %param.11) | copy-start | bytes 3145732
  6.5 6.9 %copy-start.4 = (f32[2,1024]{1,0:T(2,128)S(1)}, f32[2,1024]{1,0:T(2,128)}, u32[]{:S(2)}) copy-start(f32[2,1024]{1,0:T(2,128)} %param.12) | copy-start | bytes 24580
  6.5 109.3 %all-gather.2.cloned.1.call-start = ((), (), s32[]{:S(2)}) async-start(), calls=%async_computation | async-start | bytes 4456448 | tf_op jit(solution)/shard_map/all_gather | solution.py:74
  13.8 6.4 %copy-start.3 = (bf16[2,256,1024]{2,1,0:T(8,128)(2,1)}, bf16[2,256,1024]{2,1,0:T(8,128)(2,1)S(1)}, u32[]{:S(2)}) copy-start(bf16[2,256,1024]{2,1,0:T(8,128)(2,1)S(1)} %fusion.36) | copy-start | bytes 3145732
  13.8 9.0 %copy-start.9 = (s32[2]{0:T(128)S(1)}, s32[2]{0:T(128)}, u32[]{:S(2)}) copy-start(s32[2]{0:T(128)} %param.20) | copy-start | bytes 28
  13.8 9.0 %copy-start.6 = (s32[2,4]{1,0:T(2,128)S(1)}, s32[2,4]{1,0:T(2,128)}, u32[]{:S(2)}) copy-start(s32[2,4]{1,0:T(2,128)} %param.19) | copy-start | bytes 100
  13.8 9.3 %copy-start.10 = (s32[2]{0:T(128)S(1)}, s32[2]{0:T(128)}, u32[]{:S(2)}) copy-start(s32[2]{0:T(128)} %param.18) | copy-start | bytes 28
  13.8 9.4 %copy-start.5 = (s32[2,5]{1,0:T(2,128)S(1)}, s32[2,5]{1,0:T(2,128)}, u32[]{:S(2)}) copy-start(s32[2,5]{1,0:T(2,128)} %param.17) | copy-start | bytes 124
  20.2 63.2 %collective-permute-start.1 = (bf16[2,256,2048]{2,1,0:T(8,128)(2,1)}, bf16[2,256,2048]{2,1,0:T(8,128)(2,1)}, u32[]{:S(2)}, u32[]{:S(2)}) collective-permute-start(bf16[2,256,2048]{2,1,0:T(8,128)(2,1)} %bitcast.1), channel_id=1, source_target_pairs={{1,0},{2,1},{3,2},{4,3},{5,4},{6,5},{7,6},{8,7},{9,8},{10,9},{11,1... | collective-permute-start | bytes 6291464 | tf_op jit(solution)/shard_map/ppermute | solution.py:17
  20.2 63.1 %collective-permute-start = (bf16[2,256,2048]{2,1,0:T(8,128)(2,1)}, bf16[2,256,2048]{2,1,0:T(8,128)(2,1)}, u32[]{:S(2)}, u32[]{:S(2)}) collective-permute-start(bf16[2,256,2048]{2,1,0:T(8,128)(2,1)} %bitcast.1), channel_id=1, source_target_pairs={{0,1},{1,2},{2,3},{3,4},{4,5},{5,6},{6,7},{7,8},{8,9},{9,10},{10,1... | collective-permute-start | bytes 6291464 | tf_op jit(solution)/shard_map/ppermute | solution.py:16
  23.6 3.2 %copy-start.7 = (s32[4]{0:T(128)S(1)}, s32[4]{0:T(128)}, u32[]{:S(2)}) copy-start(s32[4]{0:T(128)} %param.21) | copy-start | bytes 52
  233.5 10.6 %copy-start.8 = (bf16[1024,1024]{1,0:T(8,128)(2,1)S(1)}, bf16[1024,1024]{1,0:T(8,128)(2,1)}, u32[]{:S(2)}) copy-start(bf16[1024,1024]{1,0:T(8,128)(2,1)} %param.16) | copy-start | bytes 6291460
  233.5 12.9 %copy-start.1 = (bf16[1024,1024]{1,0:T(8,128)(2,1)S(1)}, bf16[1024,1024]{1,0:T(8,128)(2,1)}, u32[]{:S(2)}) copy-start(bf16[1024,1024]{1,0:T(8,128)(2,1)} %param.14) | copy-start | bytes 6291460
Sparse Core Ops, SparseCore 0:
  12.9 79.5 all-gather.1
where the time goes:
time: 254 us; the launch traced here: 253 us
  matrix products  99.2 us (39%)
  waiting for transfers between devices  56.4 us (22%)
  local copies, waits for them, and re-layouts  54.7 us (22%)
  other arithmetic  26.5 us (10%)
  between operations  13.7 us (5%)
  starting transfers between devices  2.63 us (1%)
    ppermute x1, waiting for transfers between devices, with_halo(): after = lax.ppermute(leading, axis, down)  56.4 us
    sub x4, matrix products, attend_group(): weights = jnp.exp(scores - top)  43.7 us
    dot_general x4, matrix products, attend_group(): jnp.einsum('bhqk,bkhd->bqhd', probs, v_heads, preferred_element_type=jnp....  40.6 us
    concatenate x1, other arithmetic, shards(): keys_all = jnp.concatenate([windows, obs_all], axis=1)  16.1 us
    another operation x2, local copies, waits for them, and re-layouts, shards(): jnp.stack([window_kv[index:index + slots] for index in range(view_dev)])  15.8 us
    slice x1, local copies, waits for them, and re-layouts, shards(): keys_all[:, :, low:low + group_cols]  13.4 us
    slice x1, local copies, waits for them, and re-layouts, shards(): window_kv[index:index + slots]  10.3 us
    broadcast_in_dim x1, local copies, waits for them, and re-layouts, shards(): obs_all = jnp.broadcast_to(obs_keyval[None], (view_dev,) + obs_keyval.shape)  6.75 us
  transfers between devices with their start and end apart: 3, of which 1 were waited for; matrix products, arithmetic and copies ran while one was open for 17% of the time, Pallas kernels for 0%

commit v1 on v0

v1 whole, which is shorter than its diff:
```python
import functools

import jax
import jax.numpy as jnp
from jax import lax
from jax.experimental import pallas as pl
from jax.experimental.pallas import tpu as pltpu
from jax.sharding import PartitionSpec as P

HEADS = 16
LANES = 128
DEAD = -1e30


def normalize(rows):
    values = rows.astype(jnp.float32)
    centered = values - jnp.mean(values, axis=-1, keepdims=True)
    return centered * lax.rsqrt(jnp.mean(centered * centered, axis=-1, keepdims=True) + 1e-06)


def dot_t(a, b):
    return lax.dot_general(a, b, (((1,), (1,)), ((), ())), preferred_element_type=jnp.float32)


def attention_kernel(view_dev, tok, size, slots, obs_views, *refs):
    (cap_ref, q_ref, kb_ref, vb_ref, ko_ref, vo_ref, ka_ref, va_ref, kx_ref, vx_ref, w_ref,
     out_ref, s0, s1, e0, e1, m0, m1, r0, r1, heads) = refs
    step = pl.program_id(0)
    halo = slots - 1
    blocks = slots + obs_views

    def key_block(view, j, key):
        before, own, after, obs = (
            (kb_ref, ko_ref, ka_ref, kx_ref) if key else (vb_ref, vo_ref, va_ref, vx_ref)
        )
        if j >= slots:
            return obs[pl.ds((j - slots) * tok, tok), :]
        place = view + j
        reach = halo // 2
        if place < reach:
            return before[pl.ds(place * tok, tok), :]
        if place < reach + view_dev:
            return own[pl.ds((place - reach) * tok, tok), :]
        return after[pl.ds((place - reach - view_dev) * tok, tok), :]

    lane = lax.broadcasted_iota(jnp.int32, (tok, LANES), 1)
    per_tile = LANES // size
    units = [(view, head) for view in range(view_dev) for head in range(per_tile)]
    score, expo, top, inv = (s0, s1), (e0, e1), (m0, m1), (r0, r1)
    total = [None] * len(units)
    mixed = [None] * view_dev
    tiles = tok // LANES
    for t in range(len(units) + 2):
        a, b, c = t, t - 1, t - 2
        if a < len(units):
            view, head = units[a]
            q_all = q_ref[pl.ds(view * tok, tok), :]
            mine = (lane >= head * size) & (lane < (head + 1) * size)
            q = jnp.where(mine, q_all.astype(jnp.float32) * size ** -0.5, 0.0).astype(jnp.bfloat16)
            high = None
        if 0 <= b < len(units):
            low = None
            m_b = top[b % 2][...]
        if 0 <= c < len(units):
            acc = None
            r_c = inv[c % 2][...]
        for j in range(blocks):
            if a < len(units):
                s = dot_t(q, key_block(view, j, True))
                s = jnp.minimum(s, cap_ref[view : view + 1, pl.ds(j * tok, tok)])
                score[a % 2][:, pl.ds(j * tok, tok)] = s
                for i in range(tiles):
                    part = s[:, i * LANES : (i + 1) * LANES]
                    high = part if high is None else jnp.maximum(high, part)
            if 0 <= b < len(units):
                for i in range(tiles):
                    cols = pl.ds(j * tok + i * LANES, LANES)
                    e = jnp.exp(score[b % 2][:, cols] - m_b)
                    expo[b % 2][:, cols] = e
                    low = e if low is None else low + e
            if 0 <= c < len(units):
                probs = jnp.concatenate(
                    [
                        (expo[c % 2][:, pl.ds(j * tok + i * LANES, LANES)] * r_c).astype(jnp.bfloat16)
                        for i in range(tiles)
                    ],
                    axis=1,
                )
                part = jnp.dot(
                    probs, key_block(units[c][0], j, False), preferred_element_type=jnp.float32
                )
                acc = part if acc is None else acc + part
        if a < len(units):
            top[a % 2][...] = jnp.broadcast_to(
                jnp.max(high, axis=1, keepdims=True), (tok, LANES)
            )
        if 0 <= b < len(units):
            inv[b % 2][...] = jnp.broadcast_to(
                1.0 / jnp.sum(low, axis=1, keepdims=True), (tok, LANES)
            )
        if 0 <= c < len(units):
            view_c, head_c = units[c]
            if head_c == 0:
                mixed[view_c] = acc
            else:
                mixed[view_c] = jnp.where(lane >= head_c * size, acc, mixed[view_c])
            if head_c == per_tile - 1:
                heads[pl.ds(view_c * tok, tok), pl.ds(pl.multiple_of(step * LANES, LANES), LANES)] = (
                    mixed[view_c].astype(jnp.bfloat16)
                )

    @pl.when(step == pl.num_programs(0) - 1)
    def _():
        for view in range(view_dev):
            rows = pl.ds(view * tok, tok)
            out_ref[rows, :] = jnp.dot(
                heads[rows, :], w_ref[...], preferred_element_type=jnp.float32
            ).astype(jnp.bfloat16)


def attention(cap, query, before, own, after, obs, w_out, view_dev, tok, size, slots, obs_views):
    rows, width = query.shape
    pairs = width // LANES
    keys = (slots + obs_views) * tok

    def halves(array):
        n = array.shape[0]
        return (
            pl.BlockSpec((n, LANES), lambda p: (0, p)),
            pl.BlockSpec((n, LANES), lambda p: (0, p + pairs)),
        )

    whole = lambda shape: pl.BlockSpec(shape, lambda p: (0, 0))
    return pl.pallas_call(
        functools.partial(attention_kernel, view_dev, tok, size, slots, obs_views),
        grid=(pairs,),
        in_specs=[
            whole(cap.shape),
            pl.BlockSpec((rows, LANES), lambda p: (0, p)),
            *halves(before),
            *halves(own),
            *halves(after),
            *halves(obs),
            whole(w_out.shape),
        ],
        out_specs=whole((rows, width)),
        out_shape=jax.ShapeDtypeStruct((rows, width), jnp.bfloat16),
        scratch_shapes=[
            pltpu.VMEM((tok, keys), jnp.float32),
            pltpu.VMEM((tok, keys), jnp.float32),
            pltpu.VMEM((tok, keys), jnp.float32),
            pltpu.VMEM((tok, keys), jnp.float32),
            pltpu.VMEM((tok, LANES), jnp.float32),
            pltpu.VMEM((tok, LANES), jnp.float32),
            pltpu.VMEM((tok, LANES), jnp.float32),
            pltpu.VMEM((tok, LANES), jnp.float32),
            pltpu.VMEM((rows, width), jnp.bfloat16),
        ],
        compiler_params=pltpu.CompilerParams(vmem_limit_bytes=40 * 1024 * 1024),
    )(cap, query, before, before, own, own, after, after, obs, obs, w_out)


def shards(
    latents,
    mod_scale,
    observed,
    w_query,
    w_keyval,
    w_out,
    pair_views,
    pair_count,
    cond_views,
    cond_count,
    obs_count,
):
    view_dev, tok, width = latents.shape
    slots = pair_views.shape[1]
    reach = (slots - 1) // 2
    peers = lax.axis_size("view")
    views = view_dev * peers
    first = lax.axis_index("view") * view_dev
    obs_views = obs_count.shape[0]
    obs_rows = lax.all_gather(observed, "view", axis=0, tiled=True)
    modulated = (normalize(latents) * mod_scale[:, None, :]).astype(jnp.bfloat16)
    flat = modulated.reshape(view_dev * tok, width)
    up = [(i, (i + 1) % peers) for i in range(peers)]
    down = [(j, i) for i, j in up]
    edge = reach * tok
    before = lax.ppermute(flat[flat.shape[0] - edge :], "view", up)
    after = lax.ppermute(flat[:edge], "view", down)

    def project(rows, weight):
        return jnp.dot(rows, weight, preferred_element_type=jnp.float32).astype(jnp.bfloat16)

    query = project(flat, w_query)
    own_kv = project(flat, w_keyval)
    obs_kv = project(normalize(obs_rows).astype(jnp.bfloat16), w_keyval)
    before_kv = project(before, w_keyval)
    after_kv = project(after, w_keyval)

    view_ids = first + jnp.arange(view_dev, dtype=jnp.int32)
    targets = (view_ids[:, None] + jnp.arange(slots, dtype=jnp.int32)[None, :] - reach) % views
    pair_live = jnp.arange(slots, dtype=jnp.int32)[None, :] < pair_count[:, None]
    window_live = jnp.any(
        (pair_views[:, None, :] == targets[:, :, None]) & pair_live[:, None, :], axis=-1
    )
    cond_live = jnp.arange(cond_views.shape[1], dtype=jnp.int32)[None, :] < cond_count[:, None]
    obs_ids = jnp.arange(obs_views, dtype=jnp.int32)
    obs_live = jnp.any(
        (cond_views[:, None, :] == obs_ids[None, :, None]) & cond_live[:, None, :], axis=-1
    )
    token_live = jnp.arange(tok, dtype=jnp.int32)[None, :] < obs_count[:, None]
    obs_key_live = (obs_live[:, :, None] & token_live[None, :, :]).reshape(
        view_dev, obs_views * tok
    )
    live = jnp.concatenate([jnp.repeat(window_live, tok, axis=1), obs_key_live], axis=1)
    cap = jnp.where(live, jnp.finfo(jnp.float32).max, jnp.float32(DEAD))
    out = attention(
        cap, query, before_kv, own_kv, after_kv, obs_kv, w_out,
        view_dev, tok, width // HEADS, slots, obs_views,
    )
    return out.reshape(view_dev, tok, width)


def solution(mesh):
    in_specs = (
        P(("scene", "view"), None, None),
        P(("scene", "view"), None),
        P(("scene", "view"), None),
        P(),
        P(),
        P(),
        P(("scene", "view"), None),
        P(("scene", "view")),
        P(("scene", "view"), None),
        P(("scene", "view")),
        P("scene"),
    )
    out_specs = P(("scene", "view"), None, None)
    return jax.shard_map(shards, mesh=mesh, in_specs=in_specs, out_specs=out_specs, check_vma=False)
```

time: 254 us -> 119 us (0.47)
  the two profiles are of different devices: /device:TPU:1 before, /device:TPU:0 now
where the time goes in v1:
time: 119 us; the launch traced here: 118 us
  Pallas kernels  37.5 us (32%)
  waiting for transfers between devices  27 us (23%)
  matrix products  26.2 us (22%)
  between operations  13.6 us (11%)
  other arithmetic  8 us (7%)
  starting transfers between devices  5.48 us (5%)
    pallas_call x1, Pallas kernels, attention(): pl.pallas_call(functools.partial(attention_kernel, view_dev, tok, size, s...  37.5 us
    dot_general x5, matrix products, project(): jnp.dot(rows, weight, preferred_element_type=jnp.float32)  26.2 us
    all_gather x1, waiting for transfers between devices, shards(): obs_rows = lax.all_gather(observed, 'view', axis=0, tiled=True)  22.4 us
    ppermute x1, starting transfers between devices, shards(): after = lax.ppermute(flat[:edge], 'view', down)  5.44 us
    ppermute x1, waiting for transfers between devices, shards(): after = lax.ppermute(flat[:edge], 'view', down)  4.19 us
    reduce_sum x2, other arithmetic, normalize(): centered = values - jnp.mean(values, axis=-1, keepdims=True)  3.67 us
  transfers between devices with their start and end apart: 3, of which 3 were waited for; matrix products, arithmetic and copies ran while one was open for 17% of the time, Pallas kernels for 0%

profile of v1, /device:TPU:0, one launch (start us, length us, event | category | flops | bytes accessed | tf_op | source)
XLA Modules:
  0.0 118.4 jit_solution(11514083766940914106)
XLA Ops:
  6.5 0.0 copy-start
  6.5 0.0 copy-start.13
  6.6 0.0 copy-start.8
  6.6 0.0 all-gather.2.cloned.1.call-start
  6.6 1.6 %convert_reduce_fusion.1 = f32[2,256]{1,0:T(2,128)S(1)} fusion(bf16[2,256,1024]{2,1,0:T(8,128)(2,1)} %param.11), kind=kLoop, calls=%fused_computation.11 | loop fusion | flops 1048064 | bytes 1050624 | tf_op jit(solution)/shard_map/reduce_sum | solution.py:17
  8.2 1.6 %fusion.6 = f32[2,256]{1,0:T(2,128)S(1)} fusion(bf16[2,256,1024]{2,1,0:T(8,128)(2,1)} %param.11, f32[2,256]{1,0:T(2,128)S(1)} %broadcast_multiply_fusion.1), kind=kLoop, calls=%fused_computation.14 | loop fusion | flops 2096640 | bytes 1052672 | tf_op jit(solution)/shard_map/reduce_sum | solution.py:18
  9.9 0.0 copy-done.5
  9.9 0.0 copy-done.7
  9.9 1.4 %fusion.8 = bf16[2,256,1024]{2,1,0:T(8,128)(2,1)} fusion(bf16[2,256,1024]{2,1,0:T(8,128)(2,1)S(1)} %copy-done.5, f32[2,1024]{1,0:T(2,128)S(1)} %copy-done.7, f32[2,256]{1,0:T(2,128)S(1)} %add_rsqrt_fusion.1, f32[2,256]{1,0:T(2,128)S(1)} %broadcast_multiply_fusion.1), kind=kLoop, calls=%fused_computation.16 | loop fusion | flops 2621440 | bytes 2109440 | tf_op jit(solution)/shard_map/convert_element_type | solution.py:184
  11.2 5.4 %collective-permute-start.1 = (bf16[512,1024]{1,0:T(8,128)(2,1)}, bf16[512,1024]{1,0:T(8,128)(2,1)}, u32[]{:S(2)}, u32[]{:S(2)}) collective-permute-start(bf16[512,1024]{1,0:T(8,128)(2,1)} %bitcast.1), channel_id=1, source_target_pairs={{1,0},{2,1},{3,2},{4,3},{5,4},{6,5},{7,6},{8,7},{9,8},{10,9},{11,1... | collective-permute-start | bytes 3145736 | tf_op jit(solution)/shard_map/ppermute | solution.py:190
  16.7 0.0 collective-permute-start
  16.7 0.0 all-gather.2.cloned.1.call-update
  16.7 0.0 copy-done.12
  16.7 0.1 iota_compare_fusion.1
  16.8 0.0 copy-done.9
  16.8 0.1 fusion.13
  17.0 0.1 broadcast_bitcast_fusion.1
  17.1 0.0 copy-done.13
  17.1 0.1 iota_compare_fusion.2
  17.2 0.1 and_select_fusion
  17.2 0.0 copy-done.8
  17.2 0.2 and_reduce_fusion
  17.4 0.0 copy-start.10
  17.5 6.2 %convolution_convert_fusion.2.refs_4_.refs_5_ = bf16[512,2048]{1,0:T(8,128)(2,1)} fusion(bf16[512,1024]{1,0:T(8,128)(2,1)} %bitcast.1, bf16[1024,2048]{1,0:T(8,128)(2,1)} %param.15), kind=kOutput, calls=%fused_computation.8 | convolution fusion | flops 2148532224 | bytes 7340032 | tf_op jit(solution)/shard_map/dot_general | solution.py:193
  23.6 0.1 broadcast_bitcast_fusion
  23.7 0.0 copy-done.10
  23.7 0.1 lt.67
  23.8 0.0 copy-done
  23.9 0.0 copy-start.11
  23.9 2.6 %convolution_convert_fusion.4.refs_1_ = bf16[512,1024]{1,0:T(8,128)(2,1)S(1)} fusion(bf16[512,1024]{1,0:T(8,128)(2,1)} %bitcast.1, bf16[1024,1024]{1,0:T(8,128)(2,1)S(1)} %copy-done), kind=kOutput, calls=%fused_computation.19 | convolution fusion | flops 1074266112 | bytes 4194304 | tf_op jit(solution)/shard_map/dot_general | solution.py:193
  26.5 4.2 %collective-permute-done.1 = bf16[512,1024]{1,0:T(8,128)(2,1)} collective-permute-done((bf16[512,1024]{1,0:T(8,128)(2,1)}, bf16[512,1024]{1,0:T(8,128)(2,1)}, u32[]{:S(2)}, u32[]{:S(2)}) %collective-permute-start.1) | collective-permute-done | bytes 1048608 | tf_op jit(solution)/shard_map/ppermute | solution.py:190
  30.7 0.0 copy-done.11
  30.7 4.9 %convolution_convert_fusion.1.refs_6_.refs_7_ = bf16[512,2048]{1,0:T(8,128)(2,1)} fusion(bf16[512,1024]{1,0:T(8,128)(2,1)} %collective-permute-done.1, bf16[1024,2048]{1,0:T(8,128)(2,1)S(1)} %copy-done.11), kind=kOutput, calls=%fused_computation.7 | convolution fusion | flops 2148532224 | bytes 7340032 | tf_op jit(solution)/shard_map/dot_general | solution.py:193
  35.6 0.4 collective-permute-done
  36.0 4.9 %convolution_convert_fusion.3.refs_2_.refs_3_ = bf16[512,2048]{1,0:T(8,128)(2,1)} fusion(bf16[512,1024]{1,0:T(8,128)(2,1)} %collective-permute-done, bf16[1024,2048]{1,0:T(8,128)(2,1)S(1)} %copy-done.11), kind=kOutput, calls=%fused_computation.9 | convolution fusion | flops 2148532224 | bytes 7340032 | tf_op jit(solution)/shard_map/dot_general | solution.py:193
  41.0 22.4 %all-gather.2.cloned.1.call-done = bf16[1024,1024]{1,0:T(8,128)(2,1)} async-done(((bf16[64,1024]{1,0:T(8,128)(2,1)}), bf16[1024,1024]{1,0:T(8,128)(2,1)}) %all-gather.2.cloned.1.call-update) | async-done | bytes 2097168 | tf_op jit(solution)/shard_map/all_gather | solution.py:183
  63.4 2.1 %convert_reduce_fusion = f32[1024]{0:T(1024)S(1)} fusion(bf16[1024,1024]{1,0:T(8,128)(2,1)} %all-gather.2.cloned.1.call-done), kind=kLoop, calls=%fused_computation.1 | loop fusion | flops 2096128 | bytes 2101248 | tf_op jit(solution)/shard_map/reduce_sum | solution.py:17
  65.5 0.1 copy-done.6
  65.6 0.7 fusion.2
  66.3 0.0 copy-start.1
  66.4 0.0 copy-start.2
  66.4 0.0 copy-start.4
  66.4 7.6 %convolution_convert_fusion.refs_8_.refs_9_ = bf16[1024,2048]{1,0:T(8,128)(2,1)S(1)} fusion(bf16[1024,2048]{1,0:T(8,128)(2,1)} %param.15, bf16[1024,1024]{1,0:T(8,128)(2,1)S(1)} %copy-done.6, f32[1024]{0:T(1024)S(1)} %add_rsqrt_fusion, f32[1024]{0:T(1024)S(1)} %broadcast_multiply_fusion), kind=kOutput, calls=%fused_computation.6 | convolution fusion | flops 4301258752 | bytes 10493952 | tf_op jit(solution)/shard_map/dot_general | solution.py:193
  74.0 0.0 copy-done.1
  74.0 0.0 copy-done.2
  74.0 0.0 copy-done.3
  74.0 0.0 copy-done.4
  74.0 37.5 %shard_map.109 = bf16[512,1024]{1,0:T(8,128)(2,1)} custom-call(f32[2,2304]{1,0:T(2,128)S(1)} %add_select_fusion.refs_0_, bf16[512,1024]{1,0:T(8,128)(2,1)S(1)} %convolution_convert_fusion.4.refs_1_, bf16[512,2048]{1,0:T(8,128)(2,1)S(1)} %copy-done.3, bf16[512,2048]{1,0:T(8,128)(2,1)S(1)} %copy-done.3, bf16[512,2048]{1,0:T(8,128)(2,1)S(1)} %copy-done.1, ...), custom_call_target="tpu_custom_call" | custom-call | tf_op jit(solution)/shard_map/pallas_call | solution.py:134
  (18 shorter events, 0.1 us)
Async XLA Ops:
  6.5 17.3 %copy-start = (bf16[1024,1024]{1,0:T(8,128)(2,1)S(1)}, bf16[1024,1024]{1,0:T(8,128)(2,1)}, u32[]{:S(2)}) copy-start(bf16[1024,1024]{1,0:T(8,128)(2,1)} %param.14) | copy-start | bytes 6291460
  6.5 3.3 %copy-start.5 = (bf16[2,256,1024]{2,1,0:T(8,128)(2,1)S(1)}, bf16[2,256,1024]{2,1,0:T(8,128)(2,1)}, u32[]{:S(2)}) copy-start(bf16[2,256,1024]{2,1,0:T(8,128)(2,1)} %param.11) | copy-start | bytes 3145732
  6.5 3.3 %copy-start.7 = (f32[2,1024]{1,0:T(2,128)S(1)}, f32[2,1024]{1,0:T(2,128)}, u32[]{:S(2)}) copy-start(f32[2,1024]{1,0:T(2,128)} %param.12) | copy-start | bytes 24580
  6.5 10.2 %copy-start.12 = (s32[2]{0:T(128)S(1)}, s32[2]{0:T(128)}, u32[]{:S(2)}) copy-start(s32[2]{0:T(128)} %param.20) | copy-start | bytes 28
  6.5 10.3 %copy-start.9 = (s32[2,4]{1,0:T(2,128)S(1)}, s32[2,4]{1,0:T(2,128)}, u32[]{:S(2)}) copy-start(s32[2,4]{1,0:T(2,128)} %param.19) | copy-start | bytes 100
  6.5 10.5 %copy-start.13 = (s32[2]{0:T(128)S(1)}, s32[2]{0:T(128)}, u32[]{:S(2)}) copy-start(s32[2]{0:T(128)} %param.18) | copy-start | bytes 28
  6.6 10.7 %copy-start.8 = (s32[2,5]{1,0:T(2,128)S(1)}, s32[2,5]{1,0:T(2,128)}, u32[]{:S(2)}) copy-start(s32[2,5]{1,0:T(2,128)} %param.17) | copy-start | bytes 124
  6.6 56.8 %all-gather.2.cloned.1.call-start = ((), (), s32[]{:S(2)}) async-start(), calls=%async_computation | async-start | bytes 2228224 | tf_op jit(solution)/shard_map/all_gather | solution.py:183
  11.2 19.5 %collective-permute-start.1 = (bf16[512,1024]{1,0:T(8,128)(2,1)}, bf16[512,1024]{1,0:T(8,128)(2,1)}, u32[]{:S(2)}, u32[]{:S(2)}) collective-permute-start(bf16[512,1024]{1,0:T(8,128)(2,1)} %bitcast.1), channel_id=1, source_target_pairs={{1,0},{2,1},{3,2},{4,3},{5,4},{6,5},{7,6},{8,7},{9,8},{10,9},{11,1... | collective-permute-start | bytes 3145736 | tf_op jit(solution)/shard_map/ppermute | solution.py:190
  16.7 19.4 %collective-permute-start = (bf16[512,1024]{1,0:T(8,128)(2,1)}, bf16[512,1024]{1,0:T(8,128)(2,1)}, u32[]{:S(2)}, u32[]{:S(2)}) collective-permute-start(bf16[512,1024]{1,0:T(8,128)(2,1)} %bitcast.1), channel_id=1, source_target_pairs={{0,1},{1,2},{2,3},{3,4},{4,5},{5,6},{6,7},{7,8},{8,9},{9,10},{10,1... | collective-permute-start | bytes 3145736 | tf_op jit(solution)/shard_map/ppermute | solution.py:189
  17.4 6.3 %copy-start.10 = (s32[4]{0:T(128)S(1)}, s32[4]{0:T(128)}, u32[]{:S(2)}) copy-start(s32[4]{0:T(128)} %param.21) | copy-start | bytes 52
  23.9 6.9 %copy-start.11 = (bf16[1024,2048]{1,0:T(8,128)(2,1)S(1)}, bf16[1024,2048]{1,0:T(8,128)(2,1)}, u32[]{:S(2)}) copy-start(bf16[1024,2048]{1,0:T(8,128)(2,1)} %param.15) | copy-start | bytes 12582916
  63.4 2.2 %copy-start.6 = (bf16[1024,1024]{1,0:T(8,128)(2,1)S(1)}, bf16[1024,1024]{1,0:T(8,128)(2,1)}, u32[]{:S(2)}) copy-start(bf16[1024,1024]{1,0:T(8,128)(2,1)} %all-gather.2.cloned.1.call-done) | copy-start | bytes 6291460
  66.3 7.6 %copy-start.1 = (bf16[512,2048]{1,0:T(8,128)(2,1)S(1)}, bf16[512,2048]{1,0:T(8,128)(2,1)}, u32[]{:S(2)}) copy-start(bf16[512,2048]{1,0:T(8,128)(2,1)} %convolution_convert_fusion.2.refs_4_.refs_5_) | copy-start | bytes 6291460
  66.4 7.6 %copy-start.2 = (bf16[512,2048]{1,0:T(8,128)(2,1)S(1)}, bf16[512,2048]{1,0:T(8,128)(2,1)}, u32[]{:S(2)}) copy-start(bf16[512,2048]{1,0:T(8,128)(2,1)} %convolution_convert_fusion.1.refs_6_.refs_7_) | copy-start | bytes 6291460
  66.4 7.6 %copy-start.3 = (bf16[512,2048]{1,0:T(8,128)(2,1)S(1)}, bf16[512,2048]{1,0:T(8,128)(2,1)}, u32[]{:S(2)}) copy-start(bf16[512,2048]{1,0:T(8,128)(2,1)} %convolution_convert_fusion.3.refs_2_.refs_3_) | copy-start | bytes 6291460
  66.4 7.6 %copy-start.4 = (bf16[1024,1024]{1,0:T(8,128)(2,1)S(1)}, bf16[1024,1024]{1,0:T(8,128)(2,1)}, u32[]{:S(2)}) copy-start(bf16[1024,1024]{1,0:T(8,128)(2,1)} %refs_10_.1) | copy-start | bytes 6291460
Sparse Core Ops, SparseCore 0:
  16.8 46.5 all-gather.1

commit v2 on v1

--- a/solution.py
+++ b/solution.py
@@ -160,6 +160,25 @@
     )(cap, query, before, before, own, own, after, after, obs, obs, w_out)
 
 
+def gather_halving(rows, peers):
+    bits = peers.bit_length() - 1
+    turn = ([1] if bits > 1 else []) + list(range(bits - 1, 1, -1)) + ([0] if bits > 0 else [])
+    part = rows.shape[0]
+    held = rows[None]
+    done = []
+    for bit in turn:
+        pairs = [(i, i ^ (1 << bit)) for i in range(peers)]
+        came = lax.ppermute(held, "view", pairs)
+        place = sum(1 for b in done if b < bit)
+        low = 1 << place
+        count = held.shape[0]
+        shape = (count // low, 1, low, part, rows.shape[1])
+        held = jnp.concatenate([held.reshape(shape), came.reshape(shape)], axis=1)
+        held = held.reshape(2 * count, part, rows.shape[1])
+        done.append(bit)
+    return held.reshape(-1, rows.shape[1]), list(range(peers))
+
+
 def shards(
     latents,
     mod_scale,
@@ -180,7 +199,8 @@
     views = view_dev * peers
     first = lax.axis_index("view") * view_dev
     obs_views = obs_count.shape[0]
-    obs_rows = lax.all_gather(observed, "view", axis=0, tiled=True)
+    obs_norm = normalize(observed).astype(jnp.bfloat16)
+    obs_rows, order = gather_halving(obs_norm, peers)
     modulated = (normalize(latents) * mod_scale[:, None, :]).astype(jnp.bfloat16)
     flat = modulated.reshape(view_dev * tok, width)
     up = [(i, (i + 1) % peers) for i in range(peers)]
@@ -194,7 +214,7 @@
 
     query = project(flat, w_query)
     own_kv = project(flat, w_keyval)
-    obs_kv = project(normalize(obs_rows).astype(jnp.bfloat16), w_keyval)
+    obs_kv = project(obs_rows, w_keyval)
     before_kv = project(before, w_keyval)
     after_kv = project(after, w_keyval)
 
@@ -213,6 +233,11 @@
     obs_key_live = (obs_live[:, :, None] & token_live[None, :, :]).reshape(
         view_dev, obs_views * tok
     )
+    part = observed.shape[0]
+    owner = lax.axis_index("view") ^ jnp.asarray(order, jnp.int32)
+    obs_key_live = obs_key_live.reshape(view_dev, peers, part)[:, owner, :].reshape(
+        view_dev, peers * part
+    )
     live = jnp.concatenate([jnp.repeat(window_live, tok, axis=1), obs_key_live], axis=1)
     cap = jnp.where(live, jnp.finfo(jnp.float32).max, jnp.float32(DEAD))
     out = attention(

time: 119 us -> 115 us (0.966)
  between operations: 13.6 us -> 0.29 us
  waiting for transfers between devices: 27 us -> 36.1 us
  matrix products: 26.2 us -> 19.3 us
  starting transfers between devices: 5.48 us -> 8.98 us
  local copies, waits for them, and re-layouts: 0.44 us -> 2.43 us
  other arithmetic: 8 us -> 9.56 us
    ppermute x0 -> x4, waiting for transfers between devices: none -> 36.1 us  [gather_halving(): came = lax.ppermute(held, 'view', pairs)]
    all_gather x1 -> x0, waiting for transfers between devices: 22.4 us -> none  [shards(): obs_rows = lax.all_gather(observed, 'view', axis=0, tiled=True)]
    dot_general x5, matrix products: 26.2 us -> 19.3 us  [project(): jnp.dot(rows, weight, preferred_element_type=jnp.float32)]
    ppermute x1, waiting for transfers between devices: 4.19 us -> 0.01 us  [shards(): after = lax.ppermute(flat[:edge], 'view', down)]
    ppermute x0 -> x4, starting transfers between devices: none -> 3.47 us  [gather_halving(): came = lax.ppermute(held, 'view', pairs)]
    another operation x0 -> x3, other arithmetic: none -> 2.77 us  [gather_halving(): held = jnp.concatenate([held.reshape(shape), came.reshape(shape)], axis=1)]
    reduce_sum x2, other arithmetic: 3.67 us -> 1.7 us  [normalize(): centered = values - jnp.mean(values, axis=-1, keepdims=True)]
    select_n x1, other arithmetic: 0.08 us -> 1.32 us  [shards(): (view_ids[:, None] + jnp.arange(slots, dtype=jnp.int32)[None, :] - reach)...]
  transfers between devices with their start and end apart: 3 -> 6, of which waited for: 3 -> 3; matrix products, arithmetic and copies ran while one was open for 17% -> 19% of each run, Pallas kernels for 0% -> 0%
where the time goes in v2:
time: 115 us; the launch traced here: 114 us
  Pallas kernels  37.6 us (33%)
  waiting for transfers between devices  36.1 us (31%)
  matrix products  19.3 us (17%)
  other arithmetic  9.56 us (8%)
  starting transfers between devices  8.98 us (8%)
  local copies, waits for them, and re-layouts  2.43 us (2%)
    pallas_call x1, Pallas kernels, attention(): pl.pallas_call(functools.partial(attention_kernel, view_dev, tok, size, s...  37.6 us
    ppermute x4, waiting for transfers between devices, gather_halving(): came = lax.ppermute(held, 'view', pairs)  36.1 us
    dot_general x5, matrix products, project(): jnp.dot(rows, weight, preferred_element_type=jnp.float32)  19.3 us
    ppermute x1, starting transfers between devices, shards(): after = lax.ppermute(flat[:edge], 'view', down)  5.51 us
    ppermute x4, starting transfers between devices, gather_halving(): came = lax.ppermute(held, 'view', pairs)  3.47 us
    another operation x3, other arithmetic, gather_halving(): held = jnp.concatenate([held.reshape(shape), came.reshape(shape)], axis=1)  2.77 us
  transfers between devices with their start and end apart: 6, of which 3 were waited for; matrix products, arithmetic and copies ran while one was open for 19% of the time, Pallas kernels for 0%

profile of v2, /device:TPU:0, one launch (start us, length us, event | category | flops | bytes accessed | tf_op | source)
XLA Modules:
  0.0 114.3 jit_solution(9760437553159571834)
XLA Ops:
  0.0 0.0 copy-start
  0.0 1.6 %convert_reduce_fusion = f32[2,256]{1,0:T(2,128)S(1)} fusion(bf16[2,256,1024]{2,1,0:T(8,128)(2,1)} %param.12), kind=kLoop, calls=%fused_computation.6 | loop fusion | flops 1048064 | bytes 1050624 | tf_op jit(solution)/shard_map/reduce_sum | solution.py:17
  1.6 0.0 copy-start.9
  1.6 0.0 copy-start.10
  1.6 1.6 %fusion.2 = f32[2,256]{1,0:T(2,128)S(1)} fusion(bf16[2,256,1024]{2,1,0:T(8,128)(2,1)} %param.12, f32[2,256]{1,0:T(2,128)S(1)} %broadcast_multiply_fusion), kind=kLoop, calls=%fused_computation.9 | loop fusion | flops 2096640 | bytes 1052672 | tf_op jit(solution)/shard_map/reduce_sum | solution.py:18
  3.3 0.0 copy-done.3
  3.3 0.4 fusion.4
  3.7 5.5 %collective-permute-start.1 = (bf16[512,1024]{1,0:T(8,128)(2,1)S(1)}, bf16[512,1024]{1,0:T(8,128)(2,1)}, u32[]{:S(2)}, u32[]{:S(2)}) collective-permute-start(bf16[512,1024]{1,0:T(8,128)(2,1)S(1)} %bitcast.43), channel_id=1, source_target_pairs={{1,0},{2,1},{3,2},{4,3},{5,4},{6,5},{7,6},{8,7},{9,8},{10,9},{11,1... | collective-permute-start | bytes 3145736 | tf_op jit(solution)/shard_map/ppermute | solution.py:210
  9.2 0.0 collective-permute-start
  9.2 0.1 convert_reduce_fusion.1
  9.3 0.2 fusion.7
  9.5 0.1 fusion.15
  9.7 0.1 collective-permute-start.2
  9.8 0.6 iota_add_fusion
  10.4 0.1 iota_compare_fusion.1
  10.4 0.1 fusion.12
  10.6 0.6 copy.25
  11.2 1.3 %and_select_fusion = s32[2,5]{1,0:T(2,128)} fusion(s32[2]{0:T(128)} %iota_add_fusion), kind=kLoop, calls=%fused_computation.38 | loop fusion | flops 130 | bytes 48 | tf_op jit(solution)/shard_map/jit(remainder)/select_n | solution.py:222
  12.5 0.1 lt.85
  12.6 0.1 lt.86
  12.7 5.9 %convolution_convert_fusion.2.refs_4_.refs_5_ = bf16[512,2048]{1,0:T(8,128)(2,1)} fusion(bf16[512,1024]{1,0:T(8,128)(2,1)S(1)} %bitcast.45, bf16[1024,2048]{1,0:T(8,128)(2,1)} %param.16), kind=kOutput, calls=%fused_computation.3 | convolution fusion | flops 2148532224 | bytes 7340032 | tf_op jit(solution)/shard_map/dot_general | solution.py:213
  18.6 0.1 broadcast_and_fusion
  18.7 0.1 iota_compare_fusion.2
  18.8 0.2 and_reduce_fusion
  19.0 14.5 %collective-permute-done.2 = bf16[1,64,1024]{2,1,0:T(8,128)(2,1)S(1)} collective-permute-done((bf16[1,64,1024]{2,1,0:T(8,128)(2,1)S(1)}, bf16[1,64,1024]{2,1,0:T(8,128)(2,1)S(1)}, u32[]{:S(2)}, u32[]{:S(2)}) %collective-permute-start.2) | collective-permute-done | bytes 131104 | tf_op jit(solution)/shard_map/ppermute | solution.py:171
  33.6 0.6 copy-done.5
  34.2 1.6 %fusion.10 = (bf16[1,1,2,64,1024]{4,3,2,1,0:T(8,128)(2,1)S(1)}, bf16[2,64,1024]{2,1,0:T(8,128)(2,1)}) fusion(bf16[1,1,1,64,1024]{4,3,1,2,0:T(8,128)(2,1)} %bitcast.50, bf16[1,1,1,64,1024]{4,3,1,2,0:T(8,128)(2,1)S(1)} %get-tuple-element.9), kind=kLoop, calls=%fused_computation.24 | loop fusion | flops 131072 | bytes 786432 | tf_op jit(solution)/shard_map/reshape;reshape | solution.py:176
  35.8 2.6 %collective-permute-start.3 = (bf16[2,64,1024]{2,1,0:T(8,128)(2,1)}, bf16[2,64,1024]{2,1,0:T(8,128)(2,1)}, u32[]{:S(2)}, u32[]{:S(2)}) collective-permute-start(bf16[2,64,1024]{2,1,0:T(8,128)(2,1)} %get-tuple-element.8), channel_id=1, source_target_pairs={{0,8},{1,9},{2,10},{3,11},{4,12},{5,13},{6,14},{7,15},{8,0},{9,1},... | collective-permute-start | bytes 786440 | tf_op jit(solution)/shard_map/ppermute | solution.py:171
  38.4 0.1 broadcast_bitcast_fusion
  38.5 0.6 gather_fusion
  39.1 0.1 reshape.154
  39.2 10.8 %collective-permute-done.3 = bf16[2,64,1024]{2,1,0:T(8,128)(2,1)} collective-permute-done((bf16[2,64,1024]{2,1,0:T(8,128)(2,1)}, bf16[2,64,1024]{2,1,0:T(8,128)(2,1)}, u32[]{:S(2)}, u32[]{:S(2)}) %collective-permute-start.3) | collective-permute-done | bytes 262176 | tf_op jit(solution)/shard_map/ppermute | solution.py:171
  50.0 1.0 fusion.16
  51.0 0.7 collective-permute-start.4
  51.8 1.3 %convolution_convert_fusion.4.refs_1_ = bf16[512,1024]{1,0:T(8,128)(2,1)S(1)} fusion(bf16[512,1024]{1,0:T(8,128)(2,1)S(1)} %bitcast.46, bf16[1024,1024]{1,0:T(8,128)(2,1)S(1)} %copy-done), kind=kOutput, calls=%fused_computation.13 | convolution fusion | flops 1074266112 | bytes 4194304 | tf_op jit(solution)/shard_map/dot_general | solution.py:213
  53.1 10.8 %collective-permute-done.4 = bf16[4,64,1024]{2,1,0:T(8,128)(2,1)S(1)} collective-permute-done((bf16[4,64,1024]{2,1,0:T(8,128)(2,1)S(1)}, bf16[4,64,1024]{2,1,0:T(8,128)(2,1)S(1)}, u32[]{:S(2)}, u32[]{:S(2)}) %collective-permute-start.4) | collective-permute-done | bytes 524320 | tf_op jit(solution)/shard_map/ppermute | solution.py:171
  63.9 0.1 pad_maximum_fusion.1
  64.0 0.1 collective-permute-start.5
  64.1 0.0 collective-permute-done.1
  64.1 3.6 %convolution_convert_fusion.1.refs_6_.refs_7_ = bf16[512,2048]{1,0:T(8,128)(2,1)S(1)} fusion(bf16[512,1024]{1,0:T(8,128)(2,1)} %collective-permute-done.1, bf16[1024,2048]{1,0:T(8,128)(2,1)S(1)} %copy-done.12), kind=kOutput, calls=%fused_computation.2 | convolution fusion | flops 2148532224 | bytes 7340032 | tf_op jit(solution)/shard_map/dot_general | solution.py:213
  67.7 0.0 collective-permute-done
  67.7 3.6 %convolution_convert_fusion.3.refs_2_.refs_3_ = bf16[512,2048]{1,0:T(8,128)(2,1)S(1)} fusion(bf16[512,1024]{1,0:T(8,128)(2,1)} %collective-permute-done, bf16[1024,2048]{1,0:T(8,128)(2,1)S(1)} %copy-done.12), kind=kOutput, calls=%fused_computation.4 | convolution fusion | flops 2148532224 | bytes 7340032 | tf_op jit(solution)/shard_map/dot_general | solution.py:213
  71.3 0.0 collective-permute-done.5
  71.3 0.2 pad_maximum_fusion
  71.5 0.2 copy.23
  71.7 0.0 copy-start.2
  71.7 4.9 %convolution_convert_fusion.refs_8_.refs_9_ = bf16[1024,2048]{1,0:T(8,128)(2,1)S(1)} fusion(bf16[1024,1024]{1,0:T(8,128)(2,1)S(1)} %bitcast.42, bf16[1024,2048]{1,0:T(8,128)(2,1)S(1)} %copy-done.12), kind=kOutput, calls=%fused_computation.1 | convolution fusion | flops 4297064448 | bytes 10485760 | tf_op jit(solution)/shard_map/dot_general | solution.py:213
  76.7 37.6 %shard_map.118 = bf16[512,1024]{1,0:T(8,128)(2,1)} custom-call(f32[2,2304]{1,0:T(2,128)S(1)} %add_select_fusion.refs_0_, bf16[512,1024]{1,0:T(8,128)(2,1)S(1)} %convolution_convert_fusion.4.refs_1_, bf16[512,2048]{1,0:T(8,128)(2,1)S(1)} %convolution_convert_fusion.3.refs_2_.refs_3_, bf16[512,2048]{1,0:T(8,128)(2,1)S(1)} %convolution_convert_fusion.3.refs_2_.refs_3_, ...), custom_call_target="tpu_custom_call" | custom-call | tf_op jit(solution)/shard_map/pallas_call | solution.py:134
  (37 shorter events, 0.2 us)
Async XLA Ops:
  0.0 51.8 %copy-start = (bf16[1024,1024]{1,0:T(8,128)(2,1)S(1)}, bf16[1024,1024]{1,0:T(8,128)(2,1)}, u32[]{:S(2)}) copy-start(bf16[1024,1024]{1,0:T(8,128)(2,1)} %param.15) | copy-start | bytes 6291460
  0.0 3.3 %copy-start.3 = (bf16[2,256,1024]{2,1,0:T(8,128)(2,1)S(1)}, bf16[2,256,1024]{2,1,0:T(8,128)(2,1)}, u32[]{:S(2)}) copy-start(bf16[2,256,1024]{2,1,0:T(8,128)(2,1)} %param.12) | copy-start | bytes 3145732
  0.0 3.3 %copy-start.6 = (f32[2,1024]{1,0:T(2,128)S(1)}, f32[2,1024]{1,0:T(2,128)}, u32[]{:S(2)}) copy-start(f32[2,1024]{1,0:T(2,128)} %param.13) | copy-start | bytes 24580
  0.0 9.2 %copy-start.4 = (bf16[64,1024]{1,0:T(8,128)(2,1)S(1)}, bf16[64,1024]{1,0:T(8,128)(2,1)}, u32[]{:S(2)}) copy-start(bf16[64,1024]{1,0:T(8,128)(2,1)} %param.14) | copy-start | bytes 393220
  1.6 8.8 %copy-start.13 = (s32[2]{0:T(128)S(1)}, s32[2]{0:T(128)}, u32[]{:S(2)}) copy-start(s32[2]{0:T(128)} %param.21) | copy-start | bytes 28
  1.6 8.8 %copy-start.9 = (s32[2,4]{1,0:T(2,128)S(1)}, s32[2,4]{1,0:T(2,128)}, u32[]{:S(2)}) copy-start(s32[2,4]{1,0:T(2,128)} %param.20) | copy-start | bytes 100
  1.6 10.9 %copy-start.10 = (s32[4]{0:T(128)S(1)}, s32[4]{0:T(128)}, u32[]{:S(2)}) copy-start(s32[4]{0:T(128)} %param.22) | copy-start | bytes 52
  3.7 60.4 %collective-permute-start.1 = (bf16[512,1024]{1,0:T(8,128)(2,1)S(1)}, bf16[512,1024]{1,0:T(8,128)(2,1)}, u32[]{:S(2)}, u32[]{:S(2)}) collective-permute-start(bf16[512,1024]{1,0:T(8,128)(2,1)S(1)} %bitcast.43), channel_id=1, source_target_pairs={{1,0},{2,1},{3,2},{4,3},{5,4},{6,5},{7,6},{8,7},{9,8},{10,9},{11,1... | collective-permute-start | bytes 3145736 | tf_op jit(solution)/shard_map/ppermute | solution.py:210
  9.2 58.5 %collective-permute-start = (bf16[512,1024]{1,0:T(8,128)(2,1)S(1)}, bf16[512,1024]{1,0:T(8,128)(2,1)}, u32[]{:S(2)}, u32[]{:S(2)}) collective-permute-start(bf16[512,1024]{1,0:T(8,128)(2,1)S(1)} %bitcast.44), channel_id=1, source_target_pairs={{0,1},{1,2},{2,3},{3,4},{4,5},{5,6},{6,7},{7,8},{8,9},{9,10},{10,1... | collective-permute-start | bytes 3145736 | tf_op jit(solution)/shard_map/ppermute | solution.py:209
  9.7 23.9 %collective-permute-start.2 = (bf16[1,64,1024]{2,1,0:T(8,128)(2,1)S(1)}, bf16[1,64,1024]{2,1,0:T(8,128)(2,1)S(1)}, u32[]{:S(2)}, u32[]{:S(2)}) collective-permute-start(bf16[1,64,1024]{2,1,0:T(8,128)(2,1)S(1)} %get-tuple-element.10), channel_id=1, source_target_pairs={{0,2},{1,3},{2,0},{3,1},{4,6},{5,7},{6,4},{7,5},{8,10},{9,11},{10,... | collective-permute-start | bytes 393224 | tf_op jit(solution)/shard_map/ppermute | solution.py:171
  12.7 5.9 %copy-start.11 = (pred[2,4]{0,1:T(4,128)(4,1)S(1)}, pred[2,4]{0,1:T(4,128)(4,1)}, u32[]{:S(2)}) copy-start(pred[2,4]{0,1:T(4,128)(4,1)} %copy.25) | copy-start | bytes 28
  12.7 6.1 %copy-start.14 = (s32[2]{0:T(128)S(1)}, s32[2]{0:T(128)}, u32[]{:S(2)}) copy-start(s32[2]{0:T(128)} %param.19) | copy-start | bytes 28
  12.7 6.1 %copy-start.7 = (s32[2,5]{1,0:T(2,128)S(1)}, s32[2,5]{1,0:T(2,128)}, u32[]{:S(2)}) copy-start(s32[2,5]{1,0:T(2,128)} %param.18) | copy-start | bytes 124
  12.7 6.1 %copy-start.8 = (s32[2,5]{1,0:T(2,128)S(1)}, s32[2,5]{1,0:T(2,128)}, u32[]{:S(2)}) copy-start(s32[2,5]{1,0:T(2,128)} %and_select_fusion) | copy-start | bytes 124
  33.6 0.6 copy-start.5
  35.8 14.2 %collective-permute-start.3 = (bf16[2,64,1024]{2,1,0:T(8,128)(2,1)}, bf16[2,64,1024]{2,1,0:T(8,128)(2,1)}, u32[]{:S(2)}, u32[]{:S(2)}) collective-permute-start(bf16[2,64,1024]{2,1,0:T(8,128)(2,1)} %get-tuple-element.8), channel_id=1, source_target_pairs={{0,8},{1,9},{2,10},{3,11},{4,12},{5,13},{6,14},{7,15},{8,0},{9,1},... | collective-permute-start | bytes 786440 | tf_op jit(solution)/shard_map/ppermute | solution.py:171
  51.0 12.8 %collective-permute-start.4 = (bf16[4,64,1024]{2,1,0:T(8,128)(2,1)S(1)}, bf16[4,64,1024]{2,1,0:T(8,128)(2,1)S(1)}, u32[]{:S(2)}, u32[]{:S(2)}) collective-permute-start(bf16[4,64,1024]{2,1,0:T(8,128)(2,1)S(1)} %bitcast.48), channel_id=1, source_target_pairs={{0,4},{1,5},{2,6},{3,7},{4,0},{5,1},{6,2},{7,3},{8,12},{9,13},{10,... | collective-permute-start | bytes 1572872 | tf_op jit(solution)/shard_map/ppermute | solution.py:171
  51.8 12.3 %copy-start.12 = (bf16[1024,2048]{1,0:T(8,128)(2,1)S(1)}, bf16[1024,2048]{1,0:T(8,128)(2,1)}, u32[]{:S(2)}) copy-start(bf16[1024,2048]{1,0:T(8,128)(2,1)} %param.16) | copy-start | bytes 12582916
  64.0 7.3 %collective-permute-start.5 = (bf16[8,64,1024]{2,1,0:T(8,128)(2,1)S(1)}, bf16[8,64,1024]{2,1,0:T(8,128)(2,1)S(1)}, u32[]{:S(2)}, u32[]{:S(2)}) collective-permute-start(bf16[8,64,1024]{2,1,0:T(8,128)(2,1)S(1)} %bitcast.40), channel_id=1, source_target_pairs={{0,1},{1,0},{2,3},{3,2},{4,5},{5,4},{6,7},{7,6},{8,9},{9,8},{10,11... | collective-permute-start | bytes 3145736 | tf_op jit(solution)/shard_map/ppermute | solution.py:171
  71.7 4.9 %copy-start.1 = (bf16[512,2048]{1,0:T(8,128)(2,1)S(1)}, bf16[512,2048]{1,0:T(8,128)(2,1)}, u32[]{:S(2)}) copy-start(bf16[512,2048]{1,0:T(8,128)(2,1)} %convolution_convert_fusion.2.refs_4_.refs_5_) | copy-start | bytes 6291460
  71.7 4.9 %copy-start.2 = (bf16[1024,1024]{1,0:T(8,128)(2,1)S(1)}, bf16[1024,1024]{1,0:T(8,128)(2,1)}, u32[]{:S(2)}) copy-start(bf16[1024,1024]{1,0:T(8,128)(2,1)} %refs_10_.1) | copy-start | bytes 6291460

commit v3 on v1

--- a/solution.py
+++ b/solution.py
@@ -23,25 +23,16 @@
 
 
 def attention_kernel(view_dev, tok, size, slots, obs_views, *refs):
-    (cap_ref, q_ref, kb_ref, vb_ref, ko_ref, vo_ref, ka_ref, va_ref, kx_ref, vx_ref, w_ref,
+    (cap_ref, q_ref, k_ref, v_ref, w_ref,
      out_ref, s0, s1, e0, e1, m0, m1, r0, r1, heads) = refs
     step = pl.program_id(0)
     halo = slots - 1
     blocks = slots + obs_views
 
     def key_block(view, j, key):
-        before, own, after, obs = (
-            (kb_ref, ko_ref, ka_ref, kx_ref) if key else (vb_ref, vo_ref, va_ref, vx_ref)
-        )
-        if j >= slots:
-            return obs[pl.ds((j - slots) * tok, tok), :]
-        place = view + j
-        reach = halo // 2
-        if place < reach:
-            return before[pl.ds(place * tok, tok), :]
-        if place < reach + view_dev:
-            return own[pl.ds((place - reach) * tok, tok), :]
-        return after[pl.ds((place - reach - view_dev) * tok, tok), :]
+        ref = k_ref if key else v_ref
+        place = view + j if j < slots else view_dev + halo + j - slots
+        return ref[pl.ds(place * tok, tok), :]
 
     lane = lax.broadcasted_iota(jnp.int32, (tok, LANES), 1)
     per_tile = LANES // size
@@ -118,17 +109,10 @@
             ).astype(jnp.bfloat16)
 
 
-def attention(cap, query, before, own, after, obs, w_out, view_dev, tok, size, slots, obs_views):
+def attention(cap, query, keyval, w_out, view_dev, tok, size, slots, obs_views):
     rows, width = query.shape
     pairs = width // LANES
     keys = (slots + obs_views) * tok
-
-    def halves(array):
-        n = array.shape[0]
-        return (
-            pl.BlockSpec((n, LANES), lambda p: (0, p)),
-            pl.BlockSpec((n, LANES), lambda p: (0, p + pairs)),
-        )
 
     whole = lambda shape: pl.BlockSpec(shape, lambda p: (0, 0))
     return pl.pallas_call(
@@ -137,10 +121,8 @@
         in_specs=[
             whole(cap.shape),
             pl.BlockSpec((rows, LANES), lambda p: (0, p)),
-            *halves(before),
-            *halves(own),
-            *halves(after),
-            *halves(obs),
+            pl.BlockSpec((keyval.shape[0], LANES), lambda p: (0, p)),
+            pl.BlockSpec((keyval.shape[0], LANES), lambda p: (0, p + pairs)),
             whole(w_out.shape),
         ],
         out_specs=whole((rows, width)),
@@ -157,7 +139,196 @@
             pltpu.VMEM((rows, width), jnp.bfloat16),
         ],
         compiler_params=pltpu.CompilerParams(vmem_limit_bytes=40 * 1024 * 1024),
-    )(cap, query, before, before, own, own, after, after, obs, obs, w_out)
+    )(cap, query, keyval, keyval, w_out)
+
+
+def turns(peers):
+    bits = peers.bit_length() - 1
+    return ([1] if bits > 1 else []) + list(range(bits - 1, 1, -1)) + ([0] if bits > 0 else [])
+
+
+def owners(peers):
+    turn = turns(peers)
+    return [sum(((p >> i) & 1) << bit for i, bit in enumerate(turn)) for p in range(peers)]
+
+
+def project_kernel(peers, view_dev, tok):
+    def kernel(lat_ref, mod_ref, obs_ref, wq_hbm, wkv_hbm, q_out, kv_out,
+               wq, wkv, before, after, mod_b, mod_a, obs_all, rows_x, q_s, kv_s,
+               w_sem, halo_send, halo_recv, mod_send, mod_recv, obs_send, obs_recv, out_sem):
+        me = lax.axis_index("view")
+        left = lax.rem(me + peers - 1, peers)
+        right = lax.rem(me + 1, peers)
+        turn = turns(peers)
+        partners = [me + (1 << b) - (2 << b) * lax.rem(me // (1 << b), 2) for b in turn]
+        edge, width = before.shape
+        wide = kv_s.shape[1]
+
+        loads = [
+            pltpu.make_async_copy(wkv_hbm, wkv, w_sem.at[0]),
+            pltpu.make_async_copy(wq_hbm, wq, w_sem.at[1]),
+        ]
+        for load in loads:
+            load.start()
+        obs_all[0] = obs_ref[...]
+        barrier = pltpu.get_barrier_semaphore()
+        for device in [left, right] + partners:
+            pl.semaphore_signal(
+                barrier, inc=1, device_id={"view": device}, device_id_type=pl.DeviceIdType.MESH
+            )
+        pl.semaphore_wait(barrier, 2 + len(partners))
+
+        def send(src, dst, out, into, device):
+            copy = pltpu.make_async_remote_copy(
+                src_ref=src, dst_ref=dst, send_sem=out, recv_sem=into,
+                device_id={"view": device}, device_id_type=pl.DeviceIdType.MESH,
+            )
+            copy.start()
+            return copy
+
+        def exchange(i):
+            n = 1 << i
+            return send(
+                obs_all.at[pl.ds(0, n)], obs_all.at[pl.ds(n, n)],
+                obs_send.at[i], obs_recv.at[i], partners[i],
+            )
+
+        stages = [exchange(0)]
+        mods = [
+            send(mod_ref, mod_b, mod_send.at[0], mod_recv.at[0], right),
+            send(mod_ref, mod_a, mod_send.at[1], mod_recv.at[1], left),
+        ]
+        halos = [
+            send(lat_ref, before, halo_send.at[0], halo_recv.at[0], right),
+            send(lat_ref, after, halo_send.at[1], halo_recv.at[1], left),
+        ]
+
+        def advance(upto):
+            while len(stages) < min(upto, len(turn)):
+                stages[-1].wait()
+                stages.append(exchange(len(stages)))
+
+        step = 128
+
+        def prepare(ref, mod):
+            @pl.loop(0, edge // step)
+            def _(i):
+                at = pl.ds(pl.multiple_of(i * step, step), step)
+                x = normalize(ref[at, :])
+                x = x * mod[pl.ds(i // (tok // step), 1), :]
+                rows_x[at, :] = x.astype(jnp.bfloat16)
+
+        def multiply(weight, into, row, count):
+            cols = 512
+
+            @pl.loop(0, weight.shape[1] // cols)
+            def _(i):
+                at = pl.ds(pl.multiple_of(i * cols, cols), cols)
+                into[pl.ds(row, count), at] = jnp.dot(
+                    rows_x[pl.ds(0, count), :], weight[:, at], preferred_element_type=jnp.float32
+                ).astype(jnp.bfloat16)
+
+        outs = []
+
+        def emit(row, count):
+            out = pltpu.make_async_copy(
+                kv_s.at[pl.ds(row, count)], kv_out.at[pl.ds(row, count)], out_sem.at[len(outs)]
+            )
+            out.start()
+            outs.append(out)
+
+        own = view_dev * tok
+        prepare(lat_ref, mod_ref)
+        for load in loads:
+            load.wait()
+        advance(2)
+        multiply(wkv, kv_s, edge, own)
+        emit(edge, own)
+        advance(3)
+        multiply(wq, q_s, 0, own)
+        out_q = pltpu.make_async_copy(q_s, q_out, out_sem.at[5])
+        out_q.start()
+        advance(len(turn) - 1)
+
+        part = obs_ref.shape[0]
+        half = peers // 2
+        base = own + 2 * edge
+        group = max(1, step // part)
+
+        def observed_half(which):
+            @pl.loop(0, half // group)
+            def _(i):
+                x = obs_all[pl.ds(which * half + i * group, group)].astype(jnp.float32)
+                x = x.reshape(group * part, width)
+                rows_x[pl.ds(pl.multiple_of(i * group * part, group * part), group * part), :] = (
+                    normalize(x).astype(jnp.bfloat16)
+                )
+
+            multiply(wkv, kv_s, base + which * half * part, half * part)
+            emit(base + which * half * part, half * part)
+
+        def halo(i, ref, mod, row):
+            mods[i].wait()
+            halos[i].wait()
+            prepare(ref, mod)
+            multiply(wkv, kv_s, row, edge)
+            emit(row, edge)
+
+        advance(len(turn))
+        observed_half(0)
+        halo(0, before, mod_b, 0)
+        halo(1, after, mod_a, edge + own)
+        stages[-1].wait()
+        observed_half(1)
+        for out in outs:
+            out.wait()
+        out_q.wait()
+
+    return kernel
+
+
+def project_all(latents, mod_scale, observed, w_query, w_keyval, peers, reach, tok):
+    rows, width = latents.shape
+    view_dev = rows // tok
+    edge = reach * tok
+    part = observed.shape[0]
+    total = rows + 2 * edge + peers * part
+    bits = peers.bit_length() - 1
+    vmem = pl.BlockSpec(memory_space=pltpu.VMEM)
+    hbm = pl.BlockSpec(memory_space=pl.ANY)
+    bf16 = jnp.bfloat16
+    return pl.pallas_call(
+        project_kernel(peers, view_dev, tok),
+        in_specs=[vmem, vmem, vmem, hbm, hbm],
+        out_specs=[hbm, hbm],
+        out_shape=[
+            jax.ShapeDtypeStruct((rows, width), bf16),
+            jax.ShapeDtypeStruct((total, 2 * width), bf16),
+        ],
+        scratch_shapes=[
+            pltpu.VMEM(w_query.shape, bf16),
+            pltpu.VMEM(w_keyval.shape, bf16),
+            pltpu.VMEM((edge, width), bf16),
+            pltpu.VMEM((edge, width), bf16),
+            pltpu.VMEM(mod_scale.shape, jnp.float32),
+            pltpu.VMEM(mod_scale.shape, jnp.float32),
+            pltpu.VMEM((peers, part, width), bf16),
+            pltpu.VMEM((max(rows, edge, peers * part // 2), width), bf16),
+            pltpu.VMEM((rows, width), bf16),
+            pltpu.VMEM((total, 2 * width), bf16),
+            pltpu.SemaphoreType.DMA((2,)),
+            pltpu.SemaphoreType.DMA((2,)),
+            pltpu.SemaphoreType.DMA((2,)),
+            pltpu.SemaphoreType.DMA((2,)),
+            pltpu.SemaphoreType.DMA((2,)),
+            pltpu.SemaphoreType.DMA((bits,)),
+            pltpu.SemaphoreType.DMA((bits,)),
+            pltpu.SemaphoreType.DMA((6,)),
+        ],
+        compiler_params=pltpu.CompilerParams(
+            collective_id=0, has_side_effects=True, vmem_limit_bytes=48 * 1024 * 1024
+        ),
+    )(latents, mod_scale, observed, w_query, w_keyval)
 
 
 def shards(
@@ -180,24 +351,10 @@
     views = view_dev * peers
     first = lax.axis_index("view") * view_dev
     obs_views = obs_count.shape[0]
-    obs_rows = lax.all_gather(observed, "view", axis=0, tiled=True)
-    modulated = (normalize(latents) * mod_scale[:, None, :]).astype(jnp.bfloat16)
-    flat = modulated.reshape(view_dev * tok, width)
-    up = [(i, (i + 1) % peers) for i in range(peers)]
-    down = [(j, i) for i, j in up]
-    edge = reach * tok
-    before = lax.ppermute(flat[flat.shape[0] - edge :], "view", up)
-    after = lax.ppermute(flat[:edge], "view", down)
-
-    def project(rows, weight):
-        return jnp.dot(rows, weight, preferred_element_type=jnp.float32).astype(jnp.bfloat16)
-
-    query = project(flat, w_query)
-    own_kv = project(flat, w_keyval)
-    obs_kv = project(normalize(obs_rows).astype(jnp.bfloat16), w_keyval)
-    before_kv = project(before, w_keyval)
-    after_kv = project(after, w_keyval)
-
+    query, keyval = project_all(
+        latents.reshape(view_dev * tok, width), mod_scale, observed, w_query, w_keyval,
+        peers, reach, tok,
+    )
     view_ids = first + jnp.arange(view_dev, dtype=jnp.int32)
     targets = (view_ids[:, None] + jnp.arange(slots, dtype=jnp.int32)[None, :] - reach) % views
     pair_live = jnp.arange(slots, dtype=jnp.int32)[None, :] < pair_count[:, None]
@@ -213,11 +370,15 @@
     obs_key_live = (obs_live[:, :, None] & token_live[None, :, :]).reshape(
         view_dev, obs_views * tok
     )
+    part = observed.shape[0]
+    owner = lax.axis_index("view") ^ jnp.asarray(owners(peers), jnp.int32)
+    obs_key_live = obs_key_live.reshape(view_dev, peers, part)[:, owner, :].reshape(
+        view_dev, peers * part
+    )
     live = jnp.concatenate([jnp.repeat(window_live, tok, axis=1), obs_key_live], axis=1)
     cap = jnp.where(live, jnp.finfo(jnp.float32).max, jnp.float32(DEAD))
     out = attention(
-        cap, query, before_kv, own_kv, after_kv, obs_kv, w_out,
-        view_dev, tok, width // HEADS, slots, obs_views,
+        cap, query, keyval, w_out, view_dev, tok, width // HEADS, slots, obs_views,
     )
     return out.reshape(view_dev, tok, width)
 

time: 119 us -> 115 us (0.966)
  Pallas kernels: 37.5 us -> 100 us
  waiting for transfers between devices: 27 us -> 0 us
  matrix products: 26.2 us -> 0 us
  between operations: 13.6 us -> 0.08 us
  local copies, waits for them, and re-layouts: 0.44 us -> 10.1 us
  starting transfers between devices: 5.48 us -> 0 us
  other arithmetic: 8 us -> 4.04 us
    pallas_call x0 -> x1, Pallas kernels: none -> 62.3 us  [project_all(): pl.pallas_call(project_kernel(peers, view_dev, tok), in_specs=[vmem, vmem...]
    dot_general x5 -> x0, matrix products: 26.2 us -> none  [project(): jnp.dot(rows, weight, preferred_element_type=jnp.float32)]
    all_gather x1 -> x0, waiting for transfers between devices: 22.4 us -> none  [shards(): obs_rows = lax.all_gather(observed, 'view', axis=0, tiled=True)]
    unnamed x34 -> x15, local copies, waits for them, and re-layouts: 0.37 us -> 8.58 us
    reduce_sum x4 -> x0, other arithmetic: 6 us -> none  [the longest x2 3.67 us: normalize(): centered = values - jnp.mean(values, axis=-1, keepdims=True)]
    ppermute x2 -> x0, starting transfers between devices: 5.45 us -> none  [the longest x1 5.44 us: shards(): after = lax.ppermute(flat[:edge], 'view', down)]
    ppermute x2 -> x0, waiting for transfers between devices: 4.6 us -> none  [the longest x1 4.19 us: shards(): after = lax.ppermute(flat[:edge], 'view', down)]
    convert_element_type x1 -> x0, other arithmetic: 1.35 us -> none  [shards(): (normalize(latents) * mod_scale[:, None, :]).astype(jnp.bfloat16)]
  transfers between devices with their start and end apart: 3 -> 0, of which waited for: 3 -> 0; matrix products, arithmetic and copies ran while one was open for 17% -> 0% of each run, Pallas kernels for 0% -> 0%
where the time goes in v3:
time: 115 us; the launch traced here: 114 us
  Pallas kernels  100 us (87%)
  local copies, waits for them, and re-layouts  10.1 us (9%)
  other arithmetic  4.04 us (4%)
    pallas_call x1, Pallas kernels, project_all(): pl.pallas_call(project_kernel(peers, view_dev, tok), in_specs=[vmem, vmem...  62.3 us
    pallas_call x1, Pallas kernels, attention(): pl.pallas_call(functools.partial(attention_kernel, view_dev, tok, size, s...  37.6 us
    unnamed x15, local copies, waits for them, and re-layouts  8.58 us

profile of v3, /device:TPU:0, one launch (start us, length us, event | category | flops | bytes accessed | tf_op | source)
XLA Modules:
  0.0 114.2 jit_solution(13128776535818204485)
XLA Ops:
  0.0 0.7 compare_select_fusion
  0.7 0.7 iota_compare_fusion.2
  1.4 0.7 iota_compare_fusion.1
  2.1 0.8 fusion.1
  2.9 0.1 copy.18
  3.1 0.1 and_select_fusion
  3.1 0.9 and_reduce_fusion
  4.1 0.1 broadcast_bitcast_fusion
  4.2 0.7 lt.85
  4.9 0.1 lt.86
  5.0 0.1 broadcast_and_fusion
  5.1 0.6 gather_fusion
  5.7 0.1 reshape.108
  5.8 0.0 copy-start.1
  5.8 1.6 %copy-done.1 = bf16[1024,1024]{1,0:T(8,128)(2,1)S(1)} copy-done((bf16[1024,1024]{1,0:T(8,128)(2,1)S(1)}, bf16[1024,1024]{1,0:T(8,128)(2,1)}, u32[]{:S(2)}) %copy-start.1) | copy-done | bytes 2097176
  7.4 0.0 copy-start.3
  7.4 1.2 %copy-done.3 = bf16[2,256,1024]{2,1,0:T(8,128)(2,1)S(1)} copy-done((bf16[2,256,1024]{2,1,0:T(8,128)(2,1)S(1)}, bf16[2,256,1024]{2,1,0:T(8,128)(2,1)}, u32[]{:S(2)}) %copy-start.3) | copy-done | bytes 1048600
  8.6 0.0 copy-start.4
  8.6 0.9 copy-done.4
  9.5 0.0 copy-start.5
  9.5 0.7 copy-done.5
  10.2 0.0 copy-start.2
  10.2 62.3 %shard_map.118 = (bf16[512,1024]{1,0:T(8,128)(2,1)S(1)}, bf16[2560,2048]{1,0:T(8,128)(2,1)}) custom-call(bf16[512,1024]{1,0:T(8,128)(2,1)S(1)} %bitcast.10, f32[2,1024]{1,0:T(2,128)S(1)} %copy-done.5, bf16[64,1024]{1,0:T(8,128)(2,1)S(1)} %copy-done.4, bf16[1024,1024]{1,0:T(8,128)(2,1)S(1)} %copy-done.1, bf16[1024,2048]{1,0:T(8,128)(2,1)} %wkv_hbm.1), custom_call_target="tpu_custom_call" | custom-call | tf_op jit(solution)/shard_map/pallas_call | solution.py:300
  72.5 0.0 copy-done.2
  72.5 0.0 copy-start
  72.5 4.0 %copy-done = bf16[2560,2048]{1,0:T(8,128)(2,1)S(1)} copy-done((bf16[2560,2048]{1,0:T(8,128)(2,1)S(1)}, bf16[2560,2048]{1,0:T(8,128)(2,1)}, u32[]{:S(2)}) %copy-start) | copy-done | bytes 10485784
  76.5 37.6 %shard_map.119 = bf16[512,1024]{1,0:T(8,128)(2,1)} custom-call(f32[2,2304]{1,0:T(2,128)S(1)} %add_select_fusion.refs_0_, bf16[512,1024]{1,0:T(8,128)(2,1)S(1)} %get-tuple-element.7.refs_1_, bf16[2560,2048]{1,0:T(8,128)(2,1)S(1)} %copy-done, bf16[2560,2048]{1,0:T(8,128)(2,1)S(1)} %copy-done, bf16[1024,1024]{1,0:T(8,128)(2,1)S(1)} %copy-done.2), custom_call_target="tpu_custom_call" | custom-call | tf_op jit(solution)/shard_map/pallas_call | solution.py:118
  (9 shorter events, 0.1 us)
Async XLA Ops:
  5.8 1.6 %copy-start.1 = (bf16[1024,1024]{1,0:T(8,128)(2,1)S(1)}, bf16[1024,1024]{1,0:T(8,128)(2,1)}, u32[]{:S(2)}) copy-start(bf16[1024,1024]{1,0:T(8,128)(2,1)} %wq_hbm.1) | copy-start | bytes 6291460
  7.4 1.2 %copy-start.3 = (bf16[2,256,1024]{2,1,0:T(8,128)(2,1)S(1)}, bf16[2,256,1024]{2,1,0:T(8,128)(2,1)}, u32[]{:S(2)}) copy-start(bf16[2,256,1024]{2,1,0:T(8,128)(2,1)} %param.12) | copy-start | bytes 3145732
  8.6 0.9 copy-start.4
  9.5 0.7 copy-start.5
  10.2 62.3 %copy-start.2 = (bf16[1024,1024]{1,0:T(8,128)(2,1)S(1)}, bf16[1024,1024]{1,0:T(8,128)(2,1)}, u32[]{:S(2)}) copy-start(bf16[1024,1024]{1,0:T(8,128)(2,1)} %refs_4_.1) | copy-start | bytes 6291460
  72.5 4.0 %copy-start = (bf16[2560,2048]{1,0:T(8,128)(2,1)S(1)}, bf16[2560,2048]{1,0:T(8,128)(2,1)}, u32[]{:S(2)}) copy-start(bf16[2560,2048]{1,0:T(8,128)(2,1)} %get-tuple-element.8.refs_2_.refs_3_) | copy-start | bytes 31457284

commit v4 on v3

--- a/solution.py
+++ b/solution.py
@@ -22,12 +22,43 @@
     return lax.dot_general(a, b, (((1,), (1,)), ((), ())), preferred_element_type=jnp.float32)
 
 
-def attention_kernel(view_dev, tok, size, slots, obs_views, *refs):
-    (cap_ref, q_ref, k_ref, v_ref, w_ref,
-     out_ref, s0, s1, e0, e1, m0, m1, r0, r1, heads) = refs
+def attention_kernel(peers, view_dev, tok, size, slots, obs_views, *refs):
+    (pair_ref, pair_n, cond_ref, cond_n, obs_n, q_ref, k_ref, v_ref, w_ref,
+     out_ref, cap_ref, s0, s1, e0, e1, m0, m1, r0, r1, heads) = refs
     step = pl.program_id(0)
     halo = slots - 1
     blocks = slots + obs_views
+
+    @pl.when(step == 0)
+    def _():
+        me = lax.axis_index("view")
+        views = view_dev * peers
+        keys = obs_views * tok
+        part = keys // peers
+        column = lax.broadcasted_iota(jnp.int32, (1, keys), 1)
+        slot = column // part
+        owner = jnp.full((1, keys), me, jnp.int32)
+        for i, bit in enumerate(turns(peers)):
+            owner = owner ^ (((slot >> i) & 1) << bit)
+        token = owner * part + column % part
+        high = float(jnp.finfo(jnp.float32).max)
+        for view in range(view_dev):
+            for j in range(slots):
+                target = lax.rem(me * view_dev + view + j - halo // 2 + views, views)
+                live = jnp.bool_(False)
+                for i in range(slots):
+                    live = live | ((pair_ref[view, i] == target) & (i < pair_n[view]))
+                cap_ref[view : view + 1, pl.ds(j * tok, tok)] = jnp.full(
+                    (1, tok), jnp.where(live, high, DEAD), jnp.float32
+                )
+            seen = jnp.zeros((1, keys), jnp.bool_)
+            for b in range(obs_views):
+                live = jnp.bool_(False)
+                for i in range(cond_ref.shape[1]):
+                    live = live | ((cond_ref[view, i] == b) & (i < cond_n[view]))
+                upto = b * tok + jnp.where(live, jnp.minimum(obs_n[b], tok), 0)
+                seen = seen | ((token >= b * tok) & (token < upto))
+            cap_ref[view : view + 1, pl.ds(slots * tok, keys)] = jnp.where(seen, high, DEAD)
 
     def key_block(view, j, key):
         ref = k_ref if key else v_ref
@@ -109,17 +140,17 @@
             ).astype(jnp.bfloat16)
 
 
-def attention(cap, query, keyval, w_out, view_dev, tok, size, slots, obs_views):
+def attention(lists, query, keyval, w_out, peers, view_dev, tok, size, slots, obs_views):
     rows, width = query.shape
     pairs = width // LANES
     keys = (slots + obs_views) * tok
 
     whole = lambda shape: pl.BlockSpec(shape, lambda p: (0, 0))
     return pl.pallas_call(
-        functools.partial(attention_kernel, view_dev, tok, size, slots, obs_views),
+        functools.partial(attention_kernel, peers, view_dev, tok, size, slots, obs_views),
         grid=(pairs,),
         in_specs=[
-            whole(cap.shape),
+            *[pl.BlockSpec(memory_space=pltpu.SMEM)] * len(lists),
             pl.BlockSpec((rows, LANES), lambda p: (0, p)),
             pl.BlockSpec((keyval.shape[0], LANES), lambda p: (0, p)),
             pl.BlockSpec((keyval.shape[0], LANES), lambda p: (0, p + pairs)),
@@ -128,6 +159,7 @@
         out_specs=whole((rows, width)),
         out_shape=jax.ShapeDtypeStruct((rows, width), jnp.bfloat16),
         scratch_shapes=[
+            pltpu.VMEM((view_dev, keys), jnp.float32),
             pltpu.VMEM((tok, keys), jnp.float32),
             pltpu.VMEM((tok, keys), jnp.float32),
             pltpu.VMEM((tok, keys), jnp.float32),
@@ -138,18 +170,18 @@
             pltpu.VMEM((tok, LANES), jnp.float32),
             pltpu.VMEM((rows, width), jnp.bfloat16),
         ],
-        compiler_params=pltpu.CompilerParams(vmem_limit_bytes=40 * 1024 * 1024),
-    )(cap, query, keyval, keyval, w_out)
+        compiler_params=pltpu.CompilerParams(vmem_limit_bytes=60 * 1024 * 1024),
+    )(*lists, query, keyval, keyval, w_out)
 
 
 def turns(peers):
     bits = peers.bit_length() - 1
-    return ([1] if bits > 1 else []) + list(range(bits - 1, 1, -1)) + ([0] if bits > 0 else [])
-
-
-def owners(peers):
-    turn = turns(peers)
-    return [sum(((p >> i) & 1) << bit for i, bit in enumerate(turn)) for p in range(peers)]
+    return (
+        ([bits - 1] if bits > 2 else [])
+        + ([1] if bits > 1 else [])
+        + list(range(bits - 2, 1, -1))
+        + ([0] if bits > 0 else [])
+    )
 
 
 def project_kernel(peers, view_dev, tok):
@@ -193,15 +225,24 @@
                 obs_send.at[i], obs_recv.at[i], partners[i],
             )
 
+        def halo_send_all(row, count, first):
+            at = pl.ds(row, count)
+            for i, (dst, device) in enumerate(((before, right), (after, left))):
+                halos.append(
+                    send(
+                        lat_ref.at[at], dst.at[at],
+                        halo_send.at[first + i], halo_recv.at[first + i], device,
+                    )
+                )
+
+        halos = []
         stages = [exchange(0)]
         mods = [
             send(mod_ref, mod_b, mod_send.at[0], mod_recv.at[0], right),
             send(mod_ref, mod_a, mod_send.at[1], mod_recv.at[1], left),
         ]
-        halos = [
-            send(lat_ref, before, halo_send.at[0], halo_recv.at[0], right),
-            send(lat_ref, after, halo_send.at[1], halo_recv.at[1], left),
-        ]
+        cut = edge // 2
+        halo_send_all(0, cut, 0)
 
         def advance(upto):
             while len(stages) < min(upto, len(turn)):
@@ -210,13 +251,13 @@
 
         step = 128
 
-        def prepare(ref, mod):
-            @pl.loop(0, edge // step)
+        def prepare(ref, mod, row, count):
+            @pl.loop(0, count // step)
             def _(i):
-                at = pl.ds(pl.multiple_of(i * step, step), step)
+                at = pl.ds(pl.multiple_of(row + i * step, step), step)
                 x = normalize(ref[at, :])
-                x = x * mod[pl.ds(i // (tok // step), 1), :]
-                rows_x[at, :] = x.astype(jnp.bfloat16)
+                x = x * mod[pl.ds(row // tok + i // (tok // step), 1), :]
+                rows_x[pl.ds(pl.multiple_of(i * step, step), step), :] = x.astype(jnp.bfloat16)
 
         def multiply(weight, into, row, count):
             cols = 512
@@ -238,15 +279,16 @@
             outs.append(out)
 
         own = view_dev * tok
-        prepare(lat_ref, mod_ref)
+        prepare(lat_ref, mod_ref, 0, own)
         for load in loads:
             load.wait()
         advance(2)
         multiply(wkv, kv_s, edge, own)
         emit(edge, own)
         advance(3)
+        halo_send_all(cut, edge - cut, 2)
         multiply(wq, q_s, 0, own)
-        out_q = pltpu.make_async_copy(q_s, q_out, out_sem.at[5])
+        out_q = pltpu.make_async_copy(q_s, q_out, out_sem.at[7])
         out_q.start()
         advance(len(turn) - 1)
 
@@ -267,17 +309,21 @@
             multiply(wkv, kv_s, base + which * half * part, half * part)
             emit(base + which * half * part, half * part)
 
-        def halo(i, ref, mod, row):
-            mods[i].wait()
+        def halo(i, row, count):
+            ref, mod, start = (before, mod_b, 0) if i % 2 == 0 else (after, mod_a, edge + own)
             halos[i].wait()
-            prepare(ref, mod)
-            multiply(wkv, kv_s, row, edge)
-            emit(row, edge)
-
+            prepare(ref, mod, row, count)
+            multiply(wkv, kv_s, start + row, count)
+            emit(start + row, count)
+
+        mods[0].wait()
+        mods[1].wait()
+        halo(0, 0, cut)
+        halo(1, 0, cut)
         advance(len(turn))
         observed_half(0)
-        halo(0, before, mod_b, 0)
-        halo(1, after, mod_a, edge + own)
+        halo(2, cut, edge - cut)
+        halo(3, cut, edge - cut)
         stages[-1].wait()
         observed_half(1)
         for out in outs:
@@ -295,7 +341,7 @@
     total = rows + 2 * edge + peers * part
     bits = peers.bit_length() - 1
     vmem = pl.BlockSpec(memory_space=pltpu.VMEM)
-    hbm = pl.BlockSpec(memory_space=pl.ANY)
+    hbm = pl.BlockSpec(memory_space=pltpu.HBM)
     bf16 = jnp.bfloat16
     return pl.pallas_call(
         project_kernel(peers, view_dev, tok),
@@ -317,16 +363,16 @@
             pltpu.VMEM((rows, width), bf16),
             pltpu.VMEM((total, 2 * width), bf16),
             pltpu.SemaphoreType.DMA((2,)),
-            pltpu.SemaphoreType.DMA((2,)),
-            pltpu.SemaphoreType.DMA((2,)),
+            pltpu.SemaphoreType.DMA((4,)),
+            pltpu.SemaphoreType.DMA((4,)),
             pltpu.SemaphoreType.DMA((2,)),
             pltpu.SemaphoreType.DMA((2,)),
             pltpu.SemaphoreType.DMA((bits,)),
             pltpu.SemaphoreType.DMA((bits,)),
-            pltpu.SemaphoreType.DMA((6,)),
+            pltpu.SemaphoreType.DMA((8,)),
         ],
         compiler_params=pltpu.CompilerParams(
-            collective_id=0, has_side_effects=True, vmem_limit_bytes=48 * 1024 * 1024
+            collective_id=0, has_side_effects=True, vmem_limit_bytes=60 * 1024 * 1024
         ),
     )(latents, mod_scale, observed, w_query, w_keyval)
 
@@ -348,37 +394,14 @@
     slots = pair_views.shape[1]
     reach = (slots - 1) // 2
     peers = lax.axis_size("view")
-    views = view_dev * peers
-    first = lax.axis_index("view") * view_dev
     obs_views = obs_count.shape[0]
     query, keyval = project_all(
         latents.reshape(view_dev * tok, width), mod_scale, observed, w_query, w_keyval,
         peers, reach, tok,
     )
-    view_ids = first + jnp.arange(view_dev, dtype=jnp.int32)
-    targets = (view_ids[:, None] + jnp.arange(slots, dtype=jnp.int32)[None, :] - reach) % views
-    pair_live = jnp.arange(slots, dtype=jnp.int32)[None, :] < pair_count[:, None]
-    window_live = jnp.any(
-        (pair_views[:, None, :] == targets[:, :, None]) & pair_live[:, None, :], axis=-1
-    )
-    cond_live = jnp.arange(cond_views.shape[1], dtype=jnp.int32)[None, :] < cond_count[:, None]
-    obs_ids = jnp.arange(obs_views, dtype=jnp.int32)
-    obs_live = jnp.any(
-        (cond_views[:, None, :] == obs_ids[None, :, None]) & cond_live[:, None, :], axis=-1
-    )
-    token_live = jnp.arange(tok, dtype=jnp.int32)[None, :] < obs_count[:, None]
-    obs_key_live = (obs_live[:, :, None] & token_live[None, :, :]).reshape(
-        view_dev, obs_views * tok
-    )
-    part = observed.shape[0]
-    owner = lax.axis_index("view") ^ jnp.asarray(owners(peers), jnp.int32)
-    obs_key_live = obs_key_live.reshape(view_dev, peers, part)[:, owner, :].reshape(
-        view_dev, peers * part
-    )
-    live = jnp.concatenate([jnp.repeat(window_live, tok, axis=1), obs_key_live], axis=1)
-    cap = jnp.where(live, jnp.finfo(jnp.float32).max, jnp.float32(DEAD))
     out = attention(
-        cap, query, keyval, w_out, view_dev, tok, width // HEADS, slots, obs_views,
+        (pair_views, pair_count, cond_views, cond_count, obs_count), query, keyval, w_out,
+        peers, view_dev, tok, width // HEADS, slots, obs_views,
     )
     return out.reshape(view_dev, tok, width)
 

time: 115 us -> 94 us (0.82)
  local copies, waits for them, and re-layouts: 10.1 us -> 0 us
  Pallas kernels: 100 us -> 93.8 us
  other arithmetic: 4.04 us -> 0 us
    unnamed x15 -> x0, local copies, waits for them, and re-layouts: 8.58 us -> none
    pallas_call x1, Pallas kernels: 62.3 us -> 55.9 us  [project_all(): pl.pallas_call(project_kernel(peers, view_dev, tok), in_specs=[vmem, vmem...]
    reduce_or x2 -> x0, other arithmetic: 1.72 us -> none  [the longest x1 0.9 us: shards(): jnp.any((pair_views[:, None, :] == targets[:, :, None]) & pair_live[:, No...]
    lt x4 -> x0, other arithmetic: 1.47 us -> none  [the longest x1 0.73 us: shards(): jnp.arange(slots, dtype=jnp.int32)[None, :] < pair_count[:, None]]
where the time goes in v4:
time: 94 us; the launch traced here: 93.8 us
  Pallas kernels  93.8 us (100%)
    pallas_call x1, Pallas kernels, project_all(): pl.pallas_call(project_kernel(peers, view_dev, tok), in_specs=[vmem, vmem...  55.9 us
    pallas_call x1, Pallas kernels, attention(): pl.pallas_call(functools.partial(attention_kernel, peers, view_dev, tok,...  37.9 us

profile of v4, /device:TPU:0, one launch (start us, length us, event | category | flops | bytes accessed | tf_op | source)
XLA Modules:
  0.0 93.8 jit_solution(10550531864466262659)
XLA Ops:
  0.0 55.9 %shard_map.109 = (bf16[512,1024]{1,0:T(8,128)(2,1)}, bf16[2560,2048]{1,0:T(8,128)(2,1)}) custom-call(bf16[512,1024]{1,0:T(8,128)(2,1)} %bitcast.2, f32[2,1024]{1,0:T(2,128)} %mod_ref.1, bf16[64,1024]{1,0:T(8,128)(2,1)} %obs_ref.1, bf16[1024,1024]{1,0:T(8,128)(2,1)} %wq_hbm.1, bf16[1024,2048]{1,0:T(8,128)(2,1)} %wkv_hbm.1), custom_call_target="tpu_custom_call" | custom-call | tf_op jit(solution)/shard_map/pallas_call | solution.py:346
  55.9 37.9 %shard_map.110 = bf16[512,1024]{1,0:T(8,128)(2,1)} custom-call(s32[2,5]{1,0:T(2,128)} %refs_0_.1, s32[2]{0:T(128)} %refs_1_.1, s32[2,4]{1,0:T(2,128)} %refs_2_.1, s32[2]{0:T(128)} %refs_3_.1, s32[4]{0:T(128)} %refs_4_.1, bf16[512,1024]{1,0:T(8,128)(2,1)} %get-tuple-element.7.refs_5_, bf16[2560,2048]{1,0:T(8,128)(2,1)} %get-tuple-element.8.refs_6_.refs_7_, ...), custom_call_target="tpu_custom_call" | custom-call | tf_op jit(solution)/shard_map/pallas_call | solution.py:149

commit v5 on v4

--- a/solution.py
+++ b/solution.py
@@ -242,7 +242,8 @@
             send(mod_ref, mod_a, mod_send.at[1], mod_recv.at[1], left),
         ]
         cut = edge // 2
-        halo_send_all(0, cut, 0)
+        quarter = cut // 2
+        halo_send_all(0, quarter, 0)
 
         def advance(upto):
             while len(stages) < min(upto, len(turn)):
@@ -286,7 +287,8 @@
         multiply(wkv, kv_s, edge, own)
         emit(edge, own)
         advance(3)
-        halo_send_all(cut, edge - cut, 2)
+        halo_send_all(quarter, cut - quarter, 2)
+        halo_send_all(cut, edge - cut, 4)
         multiply(wq, q_s, 0, own)
         out_q = pltpu.make_async_copy(q_s, q_out, out_sem.at[7])
         out_q.start()
@@ -311,7 +313,8 @@
 
         def halo(i, row, count):
             ref, mod, start = (before, mod_b, 0) if i % 2 == 0 else (after, mod_a, edge + own)
-            halos[i].wait()
+            for copy in (halos[i], halos[i + 2]) if row == 0 else (halos[i + 2],):
+                copy.wait()
             prepare(ref, mod, row, count)
             multiply(wkv, kv_s, start + row, count)
             emit(start + row, count)
@@ -363,8 +366,8 @@
             pltpu.VMEM((rows, width), bf16),
             pltpu.VMEM((total, 2 * width), bf16),
             pltpu.SemaphoreType.DMA((2,)),
-            pltpu.SemaphoreType.DMA((4,)),
-            pltpu.SemaphoreType.DMA((4,)),
+            pltpu.SemaphoreType.DMA((6,)),
+            pltpu.SemaphoreType.DMA((6,)),
             pltpu.SemaphoreType.DMA((2,)),
             pltpu.SemaphoreType.DMA((2,)),
             pltpu.SemaphoreType.DMA((bits,)),

time: 94 us -> 96.8 us (1.030)
  Pallas kernels: 93.8 us -> 96.6 us
    pallas_call x1, Pallas kernels: 55.9 us -> 58.7 us  [project_all(): pl.pallas_call(project_kernel(peers, view_dev, tok), in_specs=[vmem, vmem...]
where the time goes in v5:
time: 96.8 us; the launch traced here: 96.6 us
  Pallas kernels  96.6 us (100%)
    pallas_call x1, Pallas kernels, project_all(): pl.pallas_call(project_kernel(peers, view_dev, tok), in_specs=[vmem, vmem...  58.7 us
    pallas_call x1, Pallas kernels, attention(): pl.pallas_call(functools.partial(attention_kernel, peers, view_dev, tok,...  37.9 us

profile of v5, /device:TPU:0, one launch (start us, length us, event | category | flops | bytes accessed | tf_op | source)
XLA Modules:
  0.0 96.6 jit_solution(4187518825204413290)
XLA Ops:
  0.0 58.7 %shard_map.109 = (bf16[512,1024]{1,0:T(8,128)(2,1)}, bf16[2560,2048]{1,0:T(8,128)(2,1)}) custom-call(bf16[512,1024]{1,0:T(8,128)(2,1)} %bitcast.2, f32[2,1024]{1,0:T(2,128)} %mod_ref.1, bf16[64,1024]{1,0:T(8,128)(2,1)} %obs_ref.1, bf16[1024,1024]{1,0:T(8,128)(2,1)} %wq_hbm.1, bf16[1024,2048]{1,0:T(8,128)(2,1)} %wkv_hbm.1), custom_call_target="tpu_custom_call" | custom-call | tf_op jit(solution)/shard_map/pallas_call | solution.py:349
  58.7 37.9 %shard_map.110 = bf16[512,1024]{1,0:T(8,128)(2,1)} custom-call(s32[2,5]{1,0:T(2,128)} %refs_0_.1, s32[2]{0:T(128)} %refs_1_.1, s32[2,4]{1,0:T(2,128)} %refs_2_.1, s32[2]{0:T(128)} %refs_3_.1, s32[4]{0:T(128)} %refs_4_.1, bf16[512,1024]{1,0:T(8,128)(2,1)} %get-tuple-element.7.refs_5_, bf16[2560,2048]{1,0:T(8,128)(2,1)} %get-tuple-element.8.refs_6_.refs_7_, ...), custom_call_target="tpu_custom_call" | custom-call | tf_op jit(solution)/shard_map/pallas_call | solution.py:149
